TPU v7x, 512 devices: a whole 4x8x8 slice. The times are simulated.
512 devices in a mesh: rows: 32 (over x, y), heads: 16 (over z, core).
Axes of the slice: x: 4, y: 8, z: 8, core: 2. Of those that a mesh axis runs over, the one named last changes fastest.
Arguments:
- queries: bfloat16 [8, 256, 4096], P(None, 'rows', 'heads'), may hold values from -6 to 6
- keys: bfloat16 [8, 256, 4096], P(None, 'rows', 'heads'), may hold values from -0.375 to 0.375
- values: bfloat16 [8, 256, 8192], P(None, 'rows', 'heads'), may hold values from -6 to 6
- gates: bfloat16 [8, 256, 8192], P(None, 'rows', 'heads'), may hold values from -6 to 6
- prefill_states: bfloat16 [256, 16, 256, 512], P('rows', 'heads'), may hold values from -0.375 to 0.375
- dest_slot: int32 [256], P('rows'), may hold values from 0 to 255, as said below
- arrive_step: int32 [256], P('rows'), may hold values from 0 to 7
- decay: float32 [16], P('heads'), may hold values from 0.3 to 0.98
- norm_gain: float32 [8192], P('heads'), may hold values from 0.1 to 1.9
- out_weight: bfloat16 [8192, 2048], P('heads'), may hold values from -0.0625 to 0.0625
Outputs:
- mixed: bfloat16 [8, 256, 2048], P(None, 'rows', 'heads')
Inputs may be any that keep to these rules, and one draw needn't show every extreme that they name: `dest_slot`: every slot is named exactly once. Request s * 8 + j (j < 8) joins a slot on index (s + j * 4) mod 32 of rows.
All inputs are finite; a program needn't handle non-finite values.
Results may differ from a plain program's by a relative error of at most 0.0049.
Values may be sent and summed in bfloat16 or wider, within the bound.
No kernel may reach another device: no remote copies, remote signals or barrier semaphores. Data moves between devices by JAX's collectives and lax.ppermute only.
A program may use at most 64 MiB of HBM per device.

v0:
```python
import jax
import jax.numpy as jnp
from jax import lax
from jax.sharding import PartitionSpec as P


def from_behind(value, axis, steps):
    count = lax.axis_size(axis)
    pairs = [(source, (source + steps) % count) for source in range(count)]
    return lax.ppermute(value, axis, pairs)


def run_rows(q_in, k_in, v_in, g_in, incoming, join_step, decay, gains):
    step_count = q_in.shape[0]
    step_ids = jnp.arange(step_count, dtype=jnp.int32)
    later = step_ids[:, None]
    earlier = step_ids[None, :]
    joined = join_step[:, None, None]
    valid = (earlier <= later) & jnp.logical_not((earlier < joined) & (joined <= later))
    gap = jnp.maximum(later - earlier, 0).astype(jnp.float32)
    powers = decay[None, :, None, None] ** gap[None, None]
    weights_mask = jnp.where(valid[:, None], powers, 0.0)
    scores = jnp.einsum("trhk,srhk->rhts", q_in, k_in, preferred_element_type=jnp.float32)
    weights = scores * weights_mask
    local_part = jnp.einsum(
        "rhts,srhv->trhv", weights, v_in.astype(jnp.float32), precision=lax.Precision.HIGHEST
    )
    since = (step_ids[:, None] - join_step[None, :] + 1).astype(jnp.float32)
    started = step_ids[:, None] >= join_step[None, :]
    carry_scale = jnp.where(
        started[:, :, None], decay[None, None, :] ** jnp.maximum(since, 0.0)[:, :, None], 0.0
    )
    carried_part = jnp.einsum(
        "trhk,rhkv->trhv", q_in.astype(jnp.float32), incoming, precision=lax.Precision.HIGHEST
    )
    readout = carry_scale[..., None] * carried_part + local_part
    inv_rms = lax.rsqrt(jnp.mean(readout * readout, axis=-1, keepdims=True) + 1e-06)
    return (readout * inv_rms * gains[None, None] * g_in.astype(jnp.float32)).astype(jnp.bfloat16)


def shards(
    queries,
    keys,
    values,
    gates,
    prefill_states,
    dest_slot,
    arrive_step,
    decay,
    norm_gain,
    out_weight,
):
    step_count = queries.shape[0]
    slot_count = queries.shape[1]
    head_count = decay.shape[0]
    key_dim = prefill_states.shape[2]
    val_dim = prefill_states.shape[3]
    all_dest, all_step = (
        lax.all_gather(dest_slot, "rows", axis=0, tiled=True),
        lax.all_gather(arrive_step, "rows", axis=0, tiled=True),
    )
    my_index = lax.axis_index("rows")
    peers = lax.axis_size("rows")
    per_source = dest_slot.shape[0]
    spacing = peers // per_source
    order_ids = jnp.arange(per_source, dtype=jnp.int32)
    sources = (my_index - order_ids * spacing) % peers
    request_ids = sources * per_source + order_ids
    local_slot = jnp.take(all_dest, request_ids) - my_index * slot_count
    step_in = jnp.take(all_step, request_ids)
    matches = local_slot[None, :] == jnp.arange(slot_count, dtype=jnp.int32)[:, None]
    join_step = jnp.sum(jnp.where(matches, step_in[None, :] + 1, 0), axis=1) - 1
    select = matches.astype(jnp.bfloat16)
    q_all = queries.reshape(step_count, slot_count, head_count, key_dim)
    k_all = keys.reshape(step_count, slot_count, head_count, key_dim)
    v_all = values.reshape(step_count, slot_count, head_count, val_dim)
    g_all = gates.reshape(step_count, slot_count, head_count, val_dim)
    gains = norm_gain.reshape(head_count, val_dim)
    arrived = []
    for order in range(per_source):
        arrived.append(from_behind(prefill_states[order], "rows", order * spacing))
    received = jnp.stack(arrived)
    incoming = jnp.einsum("rj,jhkv->rhkv", select, received, preferred_element_type=jnp.float32)
    normed = run_rows(q_all, k_all, v_all, g_all, incoming, join_step, decay, gains)
    flattened = normed.reshape(step_count * slot_count, head_count * val_dim)
    columns = out_weight.shape[1] // lax.axis_size("heads")
    own_part = lax.psum_scatter(
        lax.dot_general(
            out_weight, flattened, (((0,), (1,)), ((), ())), preferred_element_type=jnp.float32
        ),
        "heads",
        scatter_dimension=0,
        tiled=True,
    ).T
    return own_part.astype(jnp.bfloat16).reshape(step_count, slot_count, columns)


def solution(mesh):
    placed = (
        P(None, "rows", "heads"),
        P(None, "rows", "heads"),
        P(None, "rows", "heads"),
        P(None, "rows", "heads"),
        P("rows", "heads", None, None),
        P("rows"),
        P("rows"),
        P("heads"),
        P("heads"),
        P("heads", None),
    )
    return jax.shard_map(
        shards, mesh=mesh, in_specs=placed, out_specs=P(None, "rows", "heads"), check_vma=False
    )
```

profile of v0, /device:TPU:6, one launch (start us, length us, event | category | flops | bytes accessed | tf_op | source)
XLA Modules:
  0.0 165.0 jit_solution(407334200464003367)
XLA Ops:
  6.5 0.0 reduce-scatter.2.cloned.1.call-start
  6.6 2.6 %slice_bitcast_fusion = (bf16[1,256,512]{2,1,0:T(8,128)(2,1)S(1)}, bf16[1,256,512]{2,1,0:T(8,128)(2,1)S(1)}, bf16[1,256,512]{2,1,0:T(8,128)(2,1)S(1)}, bf16[1,25...) fusion(bf16[8,1,256,512]{3,2,1,0:T(8,128)(2,1)} %param.16), kind=kLoop, calls=%fused_computation.20 | loop fusion | bytes 4194304 | tf_op jit(solution)/shard_map/squeeze | solution.py:81
  9.2 2.9 %collective-permute-start = (bf16[1,256,512]{2,1,0:T(8,128)(2,1)}, bf16[1,256,512]{2,1,0:T(8,128)(2,1)}, u32[]{:S(2)}, u32[]{:S(2)}) collective-permute-start(bf16[1,256,512]{2,1,0:T(8,128)(2,1)} %get-tuple-element.14), channel_id=1, source_target_pairs={{0,0},{16,16},{32,32},{48,48},{64,64},{80,80},{96,96},{112,112},{1... | collective-permute-start | bytes 786440 | tf_op jit(solution)/shard_map/ppermute | solution.py:10
  12.1 7.7 %collective-permute-start.1 = (bf16[1,256,512]{2,1,0:T(8,128)(2,1)}, bf16[1,256,512]{2,1,0:T(8,128)(2,1)}, u32[]{:S(2)}, u32[]{:S(2)}) collective-permute-start(bf16[1,256,512]{2,1,0:T(8,128)(2,1)} %get-tuple-element.13), channel_id=1, source_target_pairs={{0,64},{16,80},{32,96},{48,112},{64,128},{80,144},{96,160},{112,17... | collective-permute-start | bytes 786440 | tf_op jit(solution)/shard_map/ppermute | solution.py:10
  19.9 2.4 %collective-permute-start.2 = (bf16[1,256,512]{2,1,0:T(8,128)(2,1)}, bf16[1,256,512]{2,1,0:T(8,128)(2,1)}, u32[]{:S(2)}, u32[]{:S(2)}) collective-permute-start(bf16[1,256,512]{2,1,0:T(8,128)(2,1)} %get-tuple-element.12), channel_id=1, source_target_pairs={{0,128},{16,144},{32,160},{48,176},{64,192},{80,208},{96,224},{112... | collective-permute-start | bytes 786440 | tf_op jit(solution)/shard_map/ppermute | solution.py:10
  22.3 3.9 %collective-permute-start.3 = (bf16[1,256,512]{2,1,0:T(8,128)(2,1)S(1)}, bf16[1,256,512]{2,1,0:T(8,128)(2,1)}, u32[]{:S(2)}, u32[]{:S(2)}) collective-permute-start(bf16[1,256,512]{2,1,0:T(8,128)(2,1)S(1)} %get-tuple-element.11), channel_id=1, source_target_pairs={{0,192},{16,208},{32,224},{48,240},{64,256},{80,272},{96,288},{112... | collective-permute-start | bytes 786440 | tf_op jit(solution)/shard_map/ppermute | solution.py:10
  26.2 8.4 %collective-permute-start.4 = (bf16[1,256,512]{2,1,0:T(8,128)(2,1)S(1)}, bf16[1,256,512]{2,1,0:T(8,128)(2,1)}, u32[]{:S(2)}, u32[]{:S(2)}) collective-permute-start(bf16[1,256,512]{2,1,0:T(8,128)(2,1)S(1)} %get-tuple-element.10), channel_id=1, source_target_pairs={{0,256},{16,272},{32,288},{48,304},{64,320},{80,336},{96,352},{112... | collective-permute-start | bytes 786440 | tf_op jit(solution)/shard_map/ppermute | solution.py:10
  34.6 1.3 dynamic-slice
  36.5 0.2 dynamic-update-slice
  36.8 0.2 dynamic-update-slice.1
  37.0 18.5 %all-reduce.2 = (s32[256]{0:T(256)S(1)}, s32[256]{0:T(256)S(1)}) all-reduce(s32[256]{0:T(256)S(1)} %dynamic-update-slice, s32[256]{0:T(256)S(1)} %dynamic-update-slice.1), channel_id=1, replica_groups=mesh['rows'=32,'heads'=16] {'rows'}, use_global_device_ids=true, to_apply=%add | all-reduce | flops 512 | bytes 4096
  55.5 0.6 gather_fusion
  56.1 0.6 gather_fusion.1
  56.8 0.1 select_reduce_fusion
  57.6 0.1 convert_power_fusion
  57.7 0.1 iota_compare_fusion.1
  57.7 0.1 copy.16
  57.8 0.0 copy-done.3
  57.8 0.1 convolution_multiply_fusion
  57.9 0.0 collective-permute-done
  57.9 7.0 %collective-permute-start.5 = (bf16[1,256,512]{2,1,0:T(8,128)(2,1)S(1)}, bf16[1,256,512]{2,1,0:T(8,128)(2,1)S(1)}, u32[]{:S(2)}, u32[]{:S(2)}) collective-permute-start(bf16[1,256,512]{2,1,0:T(8,128)(2,1)S(1)} %get-tuple-element.9), channel_id=1, source_target_pairs={{0,320},{16,336},{32,352},{48,368},{64,384},{80,400},{96,416},{112... | collective-permute-start | bytes 786440 | tf_op jit(solution)/shard_map/ppermute | solution.py:10
  65.0 1.0 bitcast_dynamic-update-slice_fusion.7
  65.9 0.0 collective-permute-done.1
  65.9 3.1 %collective-permute-start.6 = (bf16[1,256,512]{2,1,0:T(8,128)(2,1)S(1)}, bf16[1,256,512]{2,1,0:T(8,128)(2,1)S(1)}, u32[]{:S(2)}, u32[]{:S(2)}) collective-permute-start(bf16[1,256,512]{2,1,0:T(8,128)(2,1)S(1)} %get-tuple-element.15), channel_id=1, source_target_pairs={{0,384},{16,400},{32,416},{48,432},{64,448},{80,464},{96,480},{112... | collective-permute-start | bytes 786440 | tf_op jit(solution)/shard_map/ppermute | solution.py:10
  69.1 1.0 bitcast_dynamic-update-slice_fusion.6
  70.1 0.0 collective-permute-done.2
  70.1 4.5 %collective-permute-start.7 = (bf16[1,256,512]{2,1,0:T(8,128)(2,1)S(1)}, bf16[1,256,512]{2,1,0:T(8,128)(2,1)S(1)}, u32[]{:S(2)}, u32[]{:S(2)}) collective-permute-start(bf16[1,256,512]{2,1,0:T(8,128)(2,1)S(1)} %get-tuple-element.8), channel_id=1, source_target_pairs={{0,448},{16,464},{32,480},{48,496},{64,0},{80,16},{96,32},{112,48}... | collective-permute-start | bytes 786440 | tf_op jit(solution)/shard_map/ppermute | solution.py:10
  74.6 1.0 bitcast_dynamic-update-slice_fusion.5
  75.6 0.0 collective-permute-done.3
  75.6 1.0 bitcast_dynamic-update-slice_fusion.4
  76.5 0.0 collective-permute-done.4
  76.6 1.0 bitcast_dynamic-update-slice_fusion.3
  77.5 0.0 collective-permute-done.5
  77.6 0.0 collective-permute-done.6
  77.6 8.1 %collective-permute-done.7 = bf16[1,256,512]{2,1,0:T(8,128)(2,1)S(1)} collective-permute-done((bf16[1,256,512]{2,1,0:T(8,128)(2,1)S(1)}, bf16[1,256,512]{2,1,0:T(8,128)(2,1)S(1)}, u32[]{:S(2)}, u32[]{:S(2)}) %collective-permute-start.7) | collective-permute-done | bytes 262176 | tf_op jit(solution)/shard_map/ppermute | solution.py:10
  85.7 1.4 fusion.2
  87.1 0.0 copy-start.1
  87.1 0.0 copy-start.2
  87.1 0.0 copy-start.4
  87.1 3.8 %fusion.8 = f32[8,8,1,512]{3,0,1,2:T(8,128)S(1)} fusion(f32[8,256,512]{2,0,1:T(8,128)S(1)} %fusion.2, f32[8,8]{0,1:T(8,128)S(1)} %get-tuple-element.21, bf16[8,8,256]{2,1,0:T(8,128)(2,1)S(1)} %copy-done.3), kind=kOutput, calls=%fused_computation.10 | convolution fusion | flops 100696064 | bytes 4358400 | tf_op jit(solution)/shard_map/trhk,rhkv->trhv/dot_general | solution.py:33
  90.9 0.0 copy-done.1
  90.9 0.3 multiply_reduce_fusion
  91.2 0.0 copy-done.2
  91.3 0.1 fusion.11
  91.4 1.3 convolution_bitcast_fusion
  92.7 0.0 reduce-scatter.2.cloned.1.call-update
  92.7 64.1 %reduce-scatter.2.cloned.1.call-done = f32[128,64]{0,1:T(8,128)} async-done(((f32[2048,64]{0,1:T(8,128)}), f32[128,64]{0,1:T(8,128)}) %reduce-scatter.2.cloned.1.call-update) | async-done | bytes 32784 | tf_op jit(solution)/shard_map/reduce_scatter | solution.py:87
  156.8 1.4 convert_bitcast_fusion
  (21 shorter events, 0.2 us)
Async XLA Ops:
  6.5 84.8 %copy-start = (bf16[512,2048]{1,0:T(8,128)(2,1)S(1)}, bf16[512,2048]{1,0:T(8,128)(2,1)}, u32[]{:S(2)}) copy-start(bf16[512,2048]{1,0:T(8,128)(2,1)} %param.21) | copy-start | bytes 6291460
  6.5 30.0 %copy-start.6 = (s32[8]{0:T(128)S(1)}, s32[8]{0:T(128)}, u32[]{:S(2)}) copy-start(s32[8]{0:T(128)} %param.17) | copy-start | bytes 100
  6.5 30.2 %copy-start.7 = (s32[8]{0:T(128)S(1)}, s32[8]{0:T(128)}, u32[]{:S(2)}) copy-start(s32[8]{0:T(128)} %param.18) | copy-start | bytes 100
  6.5 51.3 %copy-start.3 = (bf16[8,8,256]{2,1,0:T(8,128)(2,1)S(1)}, bf16[8,8,256]{2,1,0:T(8,128)(2,1)}, u32[]{:S(2)}) copy-start(bf16[8,8,256]{2,1,0:T(8,128)(2,1)} %param.12) | copy-start | bytes 98308
  6.5 51.3 %copy-start.5 = (bf16[8,8,256]{2,1,0:T(8,128)(2,1)S(1)}, bf16[8,8,256]{2,1,0:T(8,128)(2,1)}, u32[]{:S(2)}) copy-start(bf16[8,8,256]{2,1,0:T(8,128)(2,1)} %param.13) | copy-start | bytes 98308
  6.5 150.2 %reduce-scatter.2.cloned.1.call-start = ((), (), s32[]{:S(2)}) async-start(), calls=%async_computation.1 | async-start | bytes 557056 | tf_op jit(solution)/shard_map/reduce_scatter | solution.py:87
  9.2 48.7 %collective-permute-start = (bf16[1,256,512]{2,1,0:T(8,128)(2,1)}, bf16[1,256,512]{2,1,0:T(8,128)(2,1)}, u32[]{:S(2)}, u32[]{:S(2)}) collective-permute-start(bf16[1,256,512]{2,1,0:T(8,128)(2,1)} %get-tuple-element.14), channel_id=1, source_target_pairs={{0,0},{16,16},{32,32},{48,48},{64,64},{80,80},{96,96},{112,112},{1... | collective-permute-start | bytes 786440 | tf_op jit(solution)/shard_map/ppermute | solution.py:10
  12.1 53.8 %collective-permute-start.1 = (bf16[1,256,512]{2,1,0:T(8,128)(2,1)}, bf16[1,256,512]{2,1,0:T(8,128)(2,1)}, u32[]{:S(2)}, u32[]{:S(2)}) collective-permute-start(bf16[1,256,512]{2,1,0:T(8,128)(2,1)} %get-tuple-element.13), channel_id=1, source_target_pairs={{0,64},{16,80},{32,96},{48,112},{64,128},{80,144},{96,160},{112,17... | collective-permute-start | bytes 786440 | tf_op jit(solution)/shard_map/ppermute | solution.py:10
  19.9 50.2 %collective-permute-start.2 = (bf16[1,256,512]{2,1,0:T(8,128)(2,1)}, bf16[1,256,512]{2,1,0:T(8,128)(2,1)}, u32[]{:S(2)}, u32[]{:S(2)}) collective-permute-start(bf16[1,256,512]{2,1,0:T(8,128)(2,1)} %get-tuple-element.12), channel_id=1, source_target_pairs={{0,128},{16,144},{32,160},{48,176},{64,192},{80,208},{96,224},{112... | collective-permute-start | bytes 786440 | tf_op jit(solution)/shard_map/ppermute | solution.py:10
  22.3 53.3 %collective-permute-start.3 = (bf16[1,256,512]{2,1,0:T(8,128)(2,1)S(1)}, bf16[1,256,512]{2,1,0:T(8,128)(2,1)}, u32[]{:S(2)}, u32[]{:S(2)}) collective-permute-start(bf16[1,256,512]{2,1,0:T(8,128)(2,1)S(1)} %get-tuple-element.11), channel_id=1, source_target_pairs={{0,192},{16,208},{32,224},{48,240},{64,256},{80,272},{96,288},{112... | collective-permute-start | bytes 786440 | tf_op jit(solution)/shard_map/ppermute | solution.py:10
  26.2 50.4 %collective-permute-start.4 = (bf16[1,256,512]{2,1,0:T(8,128)(2,1)S(1)}, bf16[1,256,512]{2,1,0:T(8,128)(2,1)}, u32[]{:S(2)}, u32[]{:S(2)}) collective-permute-start(bf16[1,256,512]{2,1,0:T(8,128)(2,1)S(1)} %get-tuple-element.10), channel_id=1, source_target_pairs={{0,256},{16,272},{32,288},{48,304},{64,320},{80,336},{96,352},{112... | collective-permute-start | bytes 786440 | tf_op jit(solution)/shard_map/ppermute | solution.py:10
  57.9 19.6 %collective-permute-start.5 = (bf16[1,256,512]{2,1,0:T(8,128)(2,1)S(1)}, bf16[1,256,512]{2,1,0:T(8,128)(2,1)S(1)}, u32[]{:S(2)}, u32[]{:S(2)}) collective-permute-start(bf16[1,256,512]{2,1,0:T(8,128)(2,1)S(1)} %get-tuple-element.9), channel_id=1, source_target_pairs={{0,320},{16,336},{32,352},{48,368},{64,384},{80,400},{96,416},{112... | collective-permute-start | bytes 786440 | tf_op jit(solution)/shard_map/ppermute | solution.py:10
  65.9 11.6 %collective-permute-start.6 = (bf16[1,256,512]{2,1,0:T(8,128)(2,1)S(1)}, bf16[1,256,512]{2,1,0:T(8,128)(2,1)S(1)}, u32[]{:S(2)}, u32[]{:S(2)}) collective-permute-start(bf16[1,256,512]{2,1,0:T(8,128)(2,1)S(1)} %get-tuple-element.15), channel_id=1, source_target_pairs={{0,384},{16,400},{32,416},{48,432},{64,448},{80,464},{96,480},{112... | collective-permute-start | bytes 786440 | tf_op jit(solution)/shard_map/ppermute | solution.py:10
  70.1 15.6 %collective-permute-start.7 = (bf16[1,256,512]{2,1,0:T(8,128)(2,1)S(1)}, bf16[1,256,512]{2,1,0:T(8,128)(2,1)S(1)}, u32[]{:S(2)}, u32[]{:S(2)}) collective-permute-start(bf16[1,256,512]{2,1,0:T(8,128)(2,1)S(1)} %get-tuple-element.8), channel_id=1, source_target_pairs={{0,448},{16,464},{32,480},{48,496},{64,0},{80,16},{96,32},{112,48}... | collective-permute-start | bytes 786440 | tf_op jit(solution)/shard_map/ppermute | solution.py:10
  87.1 3.9 %copy-start.1 = (bf16[8,8,512]{2,1,0:T(8,128)(2,1)S(1)}, bf16[8,8,512]{2,1,0:T(8,128)(2,1)}, u32[]{:S(2)}) copy-start(bf16[8,8,512]{2,1,0:T(8,128)(2,1)} %param.14) | copy-start | bytes 196612
  87.1 4.1 %copy-start.2 = (bf16[8,8,512]{2,1,0:T(8,128)(2,1)S(1)}, bf16[8,8,512]{2,1,0:T(8,128)(2,1)}, u32[]{:S(2)}) copy-start(bf16[8,8,512]{2,1,0:T(8,128)(2,1)} %param.15) | copy-start | bytes 196612
  87.1 4.1 %copy-start.4 = (f32[512]{0:T(512)S(1)}, f32[512]{0:T(512)}, u32[]{:S(2)}) copy-start(f32[512]{0:T(512)} %param.20) | copy-start | bytes 6148
Sparse Core Ops, SparseCore 0:
  92.8 63.9 reduce-scatter.1
where the time goes:
time: 166 us; the launch traced here: 165 us
  waiting for transfers between devices  72.2 us (43%)
  starting transfers between devices  40 us (24%)
  blocking collectives  18.5 us (11%)
  between operations  15 us (9%)
  local copies, waits for them, and re-layouts  10.7 us (6%)
  matrix products  6.91 us (4%)
  other arithmetic  1.78 us (1%)
    reduce_scatter x1, waiting for transfers between devices, shards(): lax.psum_scatter(lax.dot_general(out_weight, flattened, (((0,), (1,)), ((...  64.1 us
    ppermute x8, starting transfers between devices, from_behind(): return lax.ppermute(value, axis, pairs)  40 us
    unnamed x1, blocking collectives  18.5 us
    ppermute x8, waiting for transfers between devices, from_behind(): return lax.ppermute(value, axis, pairs)  8.08 us
    unnamed x28, local copies, waits for them, and re-layouts  6.66 us
    dot_general x1, matrix products, run_rows(): jnp.einsum('trhk,rhkv->trhv', q_in.astype(jnp.float32), incoming, precisi...  3.81 us
  transfers between devices with their start and end apart: 9, of which 2 were waited for; matrix products, arithmetic and copies ran while one was open for 5% of the time, Pallas kernels for 0%

commit v1 on v0

v1 whole, which is shorter than its diff:
```python
import jax
import jax.numpy as jnp
from jax import lax
from jax.experimental import pallas as pl
from jax.experimental.pallas import tpu as pltpu
from jax.sharding import PartitionSpec as P

F32 = jnp.float32
BF16 = jnp.bfloat16
VMEM = pl.BlockSpec(memory_space=pltpu.VMEM)
SMEM = pl.BlockSpec(memory_space=pltpu.SMEM)
PAD = 16


def int_power(base, exponent, most):
    result = jnp.ones_like(exponent, dtype=F32)
    for below in range(most):
        result = jnp.where(exponent > below, result * base, result)
    return result


def source_kernel(steps, slots, member_ref, dest_ref, step_ref, decay_ref, q_ref, state_ref, out_ref):
    peers = q_ref.shape[0]
    width = state_ref.shape[2]
    member = member_ref[0]
    decay = decay_ref[0]
    row = lax.broadcasted_iota(jnp.int32, (steps * slots, 128), 0)
    line = lax.broadcasted_iota(jnp.int32, (PAD, 128), 0)
    for peer in range(peers):
        order = lax.rem(peer - member + peers, peers)
        slot = lax.rem(dest_ref[order], slots)
        joined = step_ref[order]
        full = jnp.dot(q_ref[peer], state_ref[order], preferred_element_type=F32)
        age = lax.div(row, slots) - joined + 1
        factor = jnp.where((lax.rem(row, slots) == slot) & (age > 0), int_power(decay, age, steps), 0.0)
        for col in range(0, width, 128):
            part = full[:, col : col + 128] * factor
            part = jnp.sum(part.reshape(steps, slots, 128), axis=1)
            tail = jnp.where(line[:PAD - steps] == 0, slot if col == 0 else joined, 0).astype(F32)
            out_ref[peer, :, col : col + 128] = jnp.concatenate([part, tail], axis=0).astype(BF16)


def row_kernel(steps, slots, decay_ref, back_ref, q_ref, k_ref, v_ref, g_ref, gain_ref, w_ref, out_ref):
    rows = steps * slots
    width = v_ref.shape[1]
    decay = decay_ref[0]
    back = back_ref[...]
    lines = back.shape[0]
    head = back[:, 0:256].astype(F32)
    here = lax.broadcasted_iota(jnp.int32, (lines, lines), 0)
    there = lax.broadcasted_iota(jnp.int32, (lines, lines), 1)
    pick = here == lax.div(there, PAD) * PAD + steps
    slot_of = jnp.sum(jnp.where(pick, head[:, 0:lines], 0.0), axis=0, keepdims=True).astype(jnp.int32)
    step_of = jnp.sum(jnp.where(pick, head[:, 128 : 128 + lines], 0.0), axis=0, keepdims=True)
    row = lax.broadcasted_iota(jnp.int32, (rows, lines), 0)
    line = lax.broadcasted_iota(jnp.int32, (rows, lines), 1)
    one = (lax.rem(row, slots) == slot_of) & (lax.div(row, slots) == lax.rem(line, PAD))
    join = jnp.sum(jnp.where(one, step_of, 0.0), axis=1, keepdims=True).astype(jnp.int32)
    later = lax.broadcasted_iota(jnp.int32, (rows, rows), 0)
    earlier = lax.broadcasted_iota(jnp.int32, (rows, rows), 1)
    t_now, t_then = lax.div(later, slots), lax.div(earlier, slots)
    kept = (lax.rem(later, slots) == lax.rem(earlier, slots)) & (t_then <= t_now)
    kept = kept & ((t_then >= join) | (t_now < join))
    scores = lax.dot_general(q_ref[...], k_ref[...], (((1,), (1,)), ((), ())), preferred_element_type=F32)
    weights = jnp.where(kept, scores * int_power(decay, t_now - t_then, steps - 1), 0.0)
    coarse = weights.astype(BF16)
    fine = (weights - coarse.astype(F32)).astype(BF16)
    v = v_ref[...]
    readout = jnp.dot(jnp.where(one, 1.0, 0.0).astype(BF16), back, preferred_element_type=F32)
    readout += jnp.dot(coarse, v, preferred_element_type=F32)
    readout += jnp.dot(fine, v, preferred_element_type=F32)
    mean = jnp.sum(readout * readout, axis=1, keepdims=True) * (1.0 / width)
    normed = readout * lax.rsqrt(mean + 1e-06) * gain_ref[...] * g_ref[...].astype(F32)
    normed = normed.astype(BF16)
    shares, _, columns = out_ref.shape
    for share in range(shares):
        part = jnp.dot(normed, w_ref[:, share * columns : (share + 1) * columns], preferred_element_type=F32)
        out_ref[share] = part.astype(out_ref.dtype)


def shards(queries, keys, values, gates, prefill_states, dest_slot, arrive_step, decay, norm_gain, out_weight):
    steps, slots, key_dim = queries.shape
    val_dim = values.shape[2]
    rows = steps * slots
    per_source = dest_slot.shape[0]
    peers = lax.axis_size("rows")
    spacing = peers // per_source
    groups = [[first + spacing * m for m in range(per_source)] for first in range(spacing)]
    member = (lax.axis_index("rows") // spacing).astype(jnp.int32).reshape(1)
    q = queries.reshape(rows, key_dim)
    q_all = lax.all_to_all(
        jnp.broadcast_to(q[None], (per_source, rows, key_dim)),
        "rows", 0, 0, axis_index_groups=groups, tiled=True,
    )
    lines = per_source * PAD
    readouts = pl.pallas_call(
        lambda *refs: source_kernel(steps, slots, *refs),
        out_shape=jax.ShapeDtypeStruct((per_source, PAD, val_dim), BF16),
        in_specs=[SMEM] * 4 + [VMEM] * 2,
        out_specs=VMEM,
        compiler_params=pltpu.CompilerParams(vmem_limit_bytes=16 << 20),
        name="source_readout",
    )(member, dest_slot, arrive_step, decay, q_all, prefill_states.reshape(per_source, key_dim, val_dim))
    back = lax.all_to_all(readouts, "rows", 0, 0, axis_index_groups=groups, tiled=True)
    heads = lax.axis_size("heads")
    columns = out_weight.shape[1] // heads
    partial = pl.pallas_call(
        lambda *refs: row_kernel(steps, slots, *refs),
        out_shape=jax.ShapeDtypeStruct((heads, rows, columns), BF16),
        in_specs=[SMEM] + [VMEM] * 7,
        out_specs=VMEM,
        compiler_params=pltpu.CompilerParams(vmem_limit_bytes=16 << 20),
        name="combine_project",
    )(
        decay, back.reshape(lines, val_dim), q, keys.reshape(rows, key_dim), values.reshape(rows, val_dim),
        gates.reshape(rows, val_dim), norm_gain.reshape(1, val_dim), out_weight,
    )
    shares = lax.all_to_all(partial, "heads", 0, 0, tiled=True)
    total = jnp.sum(shares.astype(F32), axis=0)
    return total.astype(BF16).reshape(steps, slots, columns)


def solution(mesh):
    placed = (
        P(None, "rows", "heads"),
        P(None, "rows", "heads"),
        P(None, "rows", "heads"),
        P(None, "rows", "heads"),
        P("rows", "heads", None, None),
        P("rows"),
        P("rows"),
        P("heads"),
        P("heads"),
        P("heads", None),
    )
    return jax.shard_map(
        shards, mesh=mesh, in_specs=placed, out_specs=P(None, "rows", "heads"), check_vma=False
    )
```

time: 166 us -> 65.9 us (0.40)
  the two profiles are of different devices: /device:TPU:6 before, /device:TPU:9 now
where the time goes in v1:
time: 65.9 us; the launch traced here: 65.5 us
  blocking collectives  35.5 us (54%)
  waiting for transfers between devices  13.6 us (21%)
  starting transfers between devices  8.38 us (13%)
  local copies, waits for them, and re-layouts  4.54 us (7%)
  Pallas kernels  2.15 us (3%)
  between operations  0.71 us (1%)
    all_to_all x1, blocking collectives, shards(): shares = lax.all_to_all(partial, 'heads', 0, 0, tiled=True)  23.7 us
    all_to_all x1, waiting for transfers between devices, shards(): lax.all_to_all(jnp.broadcast_to(q[None], (per_source, rows, key_dim)), 'r...  13.6 us
    all_to_all x1, blocking collectives, shards(): lax.all_to_all(readouts, 'rows', 0, 0, axis_index_groups=groups, tiled=True)  11.8 us
    all_to_all x1, starting transfers between devices, shards(): lax.all_to_all(jnp.broadcast_to(q[None], (per_source, rows, key_dim)), 'r...  8.38 us
    unnamed x18, local copies, waits for them, and re-layouts  2.93 us
    broadcast_in_dim x1, local copies, waits for them, and re-layouts, shards(): jnp.broadcast_to(q[None], (per_source, rows, key_dim))  1.62 us
  transfers between devices with their start and end apart: 1, of which 1 were waited for; matrix products, arithmetic and copies ran while one was open for 0% of the time, Pallas kernels for 0%

profile of v1, /device:TPU:9, one launch (start us, length us, event | category | flops | bytes accessed | tf_op | source)
XLA Modules:
  0.0 65.5 jit_solution(7719629712140019625)
XLA Ops:
  0.0 0.0 copy-start
  0.0 1.6 %broadcast_in_dim.8 = bf16[8,64,256]{2,1,0:T(8,128)(2,1)} broadcast(bf16[64,256]{1,0:T(8,128)(2,1)} %bitcast.11), dimensions={1,2} | broadcast | bytes 294912 | tf_op jit(solution)/shard_map/broadcast_in_dim | solution.py:92
  1.6 8.4 %all-to-all-start = ((bf16[8,64,256]{2,1,0:T(8,128)(2,1)}), bf16[8,64,256]{2,1,0:T(8,128)(2,1)S(1)}, u32[]{:S(2)}, u32[]{:S(2)}) async-start(bf16[8,64,256]{2,1,0:T(8,128)(2,1)} %broadcast_in_dim.8), calls=%async_computation | async-start | bytes 524288 | tf_op jit(solution)/shard_map/all_to_all | solution.py:91
  10.7 13.6 %all-to-all-done.refs_4_ = bf16[8,64,256]{2,1,0:T(8,128)(2,1)S(1)} async-done(((bf16[8,64,256]{2,1,0:T(8,128)(2,1)}), bf16[8,64,256]{2,1,0:T(8,128)(2,1)S(1)}, u32[]{:S(2)}, u32[]{:S(2)}) %all-to-all-start) | async-done | bytes 262176 | tf_op jit(solution)/shard_map/all_to_all | solution.py:91
  24.2 0.0 copy-start.1
  24.2 1.6 %copy-done.1 = bf16[8,1,256,512]{3,2,1,0:T(8,128)(2,1)S(1)} copy-done((bf16[8,1,256,512]{3,2,1,0:T(8,128)(2,1)S(1)}, bf16[8,1,256,512]{3,2,1,0:T(8,128)(2,1)}, u32[]{:S(2)}) %copy-start.1) | copy-done | bytes 2097176
  25.8 0.0 copy-start.7
  25.8 0.7 copy-done.7
  26.5 0.0 copy-start.8
  26.5 0.7 copy-done.8
  27.1 0.0 copy-start.2
  27.1 0.0 copy-start.3
  27.1 0.0 copy-start.4
  27.1 0.0 copy-start.5
  27.1 0.0 copy-start.6
  27.1 1.3 %source_readout.1 = bf16[8,16,512]{2,1,0:T(8,128)(2,1)S(1)} custom-call(s32[1]{0:T(128)} %bitcast.refs_0_, s32[8]{0:T(128)S(1)} %copy-done.7, s32[8]{0:T(128)S(1)} %copy-done.8, f32[1]{0:T(128)S(6)} %copy.11.refs_3_.refs_0_, bf16[8,64,256]{2,1,0:T(8,128)(2,1)S(1)} %all-to-all-done.refs_4_, bf16[8,256,512]{2,1,0:T(8,128)(2,1)S(1)} %bitcast.9), custom_call_target="tpu_custom_call" | custom-call | tf_op jit(solution)/shard_map/source_readout/pallas_call | solution.py:96
  28.4 11.8 %all_to_all.15 = bf16[8,16,512]{2,1,0:T(8,128)(2,1)S(1)} all-to-all(bf16[8,16,512]{2,1,0:T(8,128)(2,1)S(1)} %source_readout.1), channel_id=1, replica_groups={{0,64,128,192,256,320,384,448},{16,80,144,208,272,336,400,464},{32,96,1..., dimensions={0} | all-to-all | bytes 262144 | tf_op jit(solution)/shard_map/all_to_all | solution.py:104
  40.3 0.0 copy-done
  40.3 0.0 copy-done.2
  40.3 0.0 copy-done.3
  40.3 0.0 copy-done.4
  40.3 0.0 copy-done.5
  40.3 0.0 copy-done.6
  40.3 0.9 %combine_project.1 = bf16[16,64,128]{2,1,0:T(8,128)(2,1)S(1)} custom-call(f32[1]{0:T(128)S(6)} %copy.11.refs_3_.refs_0_, bf16[128,512]{1,0:T(8,128)(2,1)S(1)} %bitcast.10, bf16[64,256]{1,0:T(8,128)(2,1)S(1)} %bitcast.12, bf16[64,256]{1,0:T(8,128)(2,1)S(1)} %bitcast.15, bf16[64,512]{1,0:T(8,128)(2,1)S(1)} %bitcast.13, bf16[64,512]{1,0:T(8,128)(2,1)S(1)} %bitcast.14, ...), custom_call_target="tpu_custom_call" | custom-call | tf_op jit(solution)/shard_map/combine_project/pallas_call | solution.py:107
  41.2 23.7 %all_to_all.16 = bf16[16,64,128]{2,1,0:T(8,128)(2,1)S(1)} all-to-all(bf16[16,64,128]{2,1,0:T(8,128)(2,1)S(1)} %combine_project.1), channel_id=1, replica_groups=mesh['rows'=32,'heads'=16] {'heads'}, dimensions={0} | all-to-all | bytes 524288 | tf_op jit(solution)/shard_map/all_to_all | solution.py:118
  64.9 0.6 reduce_sum.12
Async XLA Ops:
  0.0 40.3 %copy-start = (bf16[512,2048]{1,0:T(8,128)(2,1)S(1)}, bf16[512,2048]{1,0:T(8,128)(2,1)}, u32[]{:S(2)}) copy-start(bf16[512,2048]{1,0:T(8,128)(2,1)} %refs_7_.1) | copy-start | bytes 6291460
  1.6 22.6 %all-to-all-start = ((bf16[8,64,256]{2,1,0:T(8,128)(2,1)}), bf16[8,64,256]{2,1,0:T(8,128)(2,1)S(1)}, u32[]{:S(2)}, u32[]{:S(2)}) async-start(bf16[8,64,256]{2,1,0:T(8,128)(2,1)} %broadcast_in_dim.8), calls=%async_computation | async-start | bytes 524288 | tf_op jit(solution)/shard_map/all_to_all | solution.py:91
  24.2 1.6 %copy-start.1 = (bf16[8,1,256,512]{3,2,1,0:T(8,128)(2,1)S(1)}, bf16[8,1,256,512]{3,2,1,0:T(8,128)(2,1)}, u32[]{:S(2)}) copy-start(bf16[8,1,256,512]{3,2,1,0:T(8,128)(2,1)} %param.14) | copy-start | bytes 6291460
  25.8 0.7 copy-start.7
  26.5 0.7 copy-start.8
  27.1 13.1 %copy-start.2 = (bf16[8,8,256]{2,1,0:T(8,128)(2,1)S(1)}, bf16[8,8,256]{2,1,0:T(8,128)(2,1)}, u32[]{:S(2)}) copy-start(bf16[8,8,256]{2,1,0:T(8,128)(2,1)} %param.10) | copy-start | bytes 98308
  27.1 13.1 %copy-start.3 = (bf16[8,8,512]{2,1,0:T(8,128)(2,1)S(1)}, bf16[8,8,512]{2,1,0:T(8,128)(2,1)}, u32[]{:S(2)}) copy-start(bf16[8,8,512]{2,1,0:T(8,128)(2,1)} %param.12) | copy-start | bytes 196612
  27.1 13.1 %copy-start.4 = (bf16[8,8,512]{2,1,0:T(8,128)(2,1)S(1)}, bf16[8,8,512]{2,1,0:T(8,128)(2,1)}, u32[]{:S(2)}) copy-start(bf16[8,8,512]{2,1,0:T(8,128)(2,1)} %param.13) | copy-start | bytes 196612
  27.1 13.1 %copy-start.5 = (bf16[8,8,256]{2,1,0:T(8,128)(2,1)S(1)}, bf16[8,8,256]{2,1,0:T(8,128)(2,1)}, u32[]{:S(2)}) copy-start(bf16[8,8,256]{2,1,0:T(8,128)(2,1)} %param.11) | copy-start | bytes 98308
  27.1 13.2 %copy-start.6 = (f32[512]{0:T(512)S(1)}, f32[512]{0:T(512)}, u32[]{:S(2)}) copy-start(f32[512]{0:T(512)} %param.18) | copy-start | bytes 6148

commit v2 on v1

v2 whole, which is shorter than its diff:
```python
import jax
import jax.numpy as jnp
from jax import lax
from jax.experimental import pallas as pl
from jax.experimental.pallas import tpu as pltpu
from jax.sharding import PartitionSpec as P

F32 = jnp.float32
BF16 = jnp.bfloat16
VMEM = pl.BlockSpec(memory_space=pltpu.VMEM)
SMEM = pl.BlockSpec(memory_space=pltpu.SMEM)
ANY = pl.BlockSpec(memory_space=pl.ANY)
TAIL = 128


def in_hbm(value):
    return pltpu.with_memory_space_constraint(value, pltpu.HBM)


def int_power(base, exponent, most):
    result = jnp.ones_like(exponent, dtype=F32)
    for below in range(most):
        result = jnp.where(exponent > below, result * base, result)
    return result


def prepare_kernel(
    spacing, steps, slots, dest_in, step_in, decay_ref, q_in, state_in,
    spread_ref, state_ref, factor_ref, tail_ref, q_ref, dest_ref, step_ref, sems,
):
    peers = factor_ref.shape[0]
    first = pltpu.make_async_copy(q_in, q_ref, sems.at[0])
    ints = [
        pltpu.make_async_copy(dest_in, dest_ref, sems.at[1]),
        pltpu.make_async_copy(step_in, step_ref, sems.at[2]),
    ]
    copies = [first] + ints + [
        pltpu.make_async_copy(state_in.at[order], state_ref.at[order], sems.at[3 + order]) for order in range(peers)
    ]
    for copy in copies:
        copy.start()
    first.wait()
    for peer in range(peers):
        spread_ref[peer] = q_ref[...]
    for copy in ints:
        copy.wait()
    member = lax.div(lax.axis_index("rows"), spacing)
    decay = decay_ref[0]
    row = lax.broadcasted_iota(jnp.int32, (steps * slots, 128), 0)
    lane = lax.broadcasted_iota(jnp.int32, (steps, TAIL), 1)
    for order in range(peers):
        slot = lax.rem(dest_ref[order], slots)
        joined = step_ref[order]
        age = lax.div(row, slots) - joined + 1
        mine = (lax.rem(row, slots) == slot) & (age > 0)
        peer = lax.rem(member + order, peers)
        factor_ref[peer] = jnp.where(mine, int_power(decay, age, steps), 0.0)
        tail_ref[peer] = jnp.where(lane < TAIL // 2, slot, joined).astype(F32)
    for copy in copies[3:]:
        copy.wait()


def source_kernel(spacing, steps, slots, q_ref, state_ref, factor_ref, tail_ref, out_ref):
    peers, _, width = state_ref.shape
    member = lax.div(lax.axis_index("rows"), spacing)
    for peer in range(peers):
        order = lax.rem(peer - member + peers, peers)
        full = jnp.dot(q_ref[peer], state_ref[order], preferred_element_type=F32)
        factor = factor_ref[peer]
        parts = []
        for col in range(0, width, 128):
            part = full[:, col : col + 128] * factor
            parts.append(jnp.sum(part.reshape(steps, slots, 128), axis=1))
        parts.append(tail_ref[peer])
        out_ref[peer] = jnp.concatenate(parts, axis=1).astype(BF16)


def row_kernel(steps, slots, decay_ref, back_ref, q_ref, k_ref, v_ref, g_ref, gain_ref, w_ref, out_ref):
    rows = steps * slots
    width = v_ref.shape[1]
    decay = decay_ref[0]
    back = back_ref[...].astype(F32)
    lines = back.shape[0] * back.shape[1]
    back = back.reshape(lines, back.shape[2])
    here = lax.broadcasted_iota(jnp.int32, (lines, TAIL), 0)
    there = lax.broadcasted_iota(jnp.int32, (lines, TAIL), 1)
    pick = here == lax.rem(there, TAIL // 2)
    facts = jnp.sum(jnp.where(pick, back[:, width:], 0.0), axis=0, keepdims=True)
    slot_of = facts[:, 0:lines].astype(jnp.int32)
    step_of = facts[:, TAIL // 2 : TAIL // 2 + lines]
    row = lax.broadcasted_iota(jnp.int32, (rows, lines), 0)
    line = lax.broadcasted_iota(jnp.int32, (rows, lines), 1)
    one = (lax.rem(row, slots) == slot_of) & (lax.div(row, slots) == lax.rem(line, steps))
    join = jnp.sum(jnp.where(one, step_of, 0.0), axis=1, keepdims=True).astype(jnp.int32)
    later = lax.broadcasted_iota(jnp.int32, (rows, rows), 0)
    earlier = lax.broadcasted_iota(jnp.int32, (rows, rows), 1)
    t_now, t_then = lax.div(later, slots), lax.div(earlier, slots)
    kept = (lax.rem(later, slots) == lax.rem(earlier, slots)) & (t_then <= t_now)
    kept = kept & ((t_then >= join) | (t_now < join))
    scores = lax.dot_general(q_ref[...], k_ref[...], (((1,), (1,)), ((), ())), preferred_element_type=F32)
    weights = jnp.where(kept, scores * int_power(decay, t_now - t_then, steps - 1), 0.0)
    coarse = weights.astype(BF16)
    fine = (weights - coarse.astype(F32)).astype(BF16)
    v = v_ref[...]
    carried = back[:, :width].astype(BF16)
    readout = jnp.dot(jnp.where(one, 1.0, 0.0).astype(BF16), carried, preferred_element_type=F32)
    readout += jnp.dot(coarse, v, preferred_element_type=F32)
    readout += jnp.dot(fine, v, preferred_element_type=F32)
    mean = jnp.sum(readout * readout, axis=1, keepdims=True) * (1.0 / width)
    normed = readout * lax.rsqrt(mean + 1e-06) * gain_ref[...] * g_ref[...].astype(F32)
    normed = normed.astype(BF16)
    shares, _, columns = out_ref.shape
    for share in range(shares):
        part = jnp.dot(normed, w_ref[:, share * columns : (share + 1) * columns], preferred_element_type=F32)
        out_ref[share] = part.astype(out_ref.dtype)


def total_kernel(shares_ref, out_ref):
    total = shares_ref[0].astype(F32)
    for share in range(1, shares_ref.shape[0]):
        total += shares_ref[share].astype(F32)
    out_ref[...] = total.astype(out_ref.dtype)


def call(kernel, name, out_shape, in_specs, out_specs, scratch=(), cost=None):
    return pl.pallas_call(
        kernel,
        out_shape=out_shape,
        in_specs=in_specs,
        out_specs=out_specs,
        scratch_shapes=scratch,
        compiler_params=pltpu.CompilerParams(vmem_limit_bytes=16 << 20),
        cost_estimate=cost,
        name=name,
    )


def shards(queries, keys, values, gates, prefill_states, dest_slot, arrive_step, decay, norm_gain, out_weight):
    steps, slots, key_dim = queries.shape
    val_dim = values.shape[2]
    rows = steps * slots
    per_source = dest_slot.shape[0]
    spacing = lax.axis_size("rows") // per_source
    groups = [[first + spacing * m for m in range(per_source)] for first in range(spacing)]
    shape = jax.ShapeDtypeStruct
    q = queries.reshape(rows, key_dim)
    states = prefill_states.reshape(per_source, key_dim, val_dim)
    spread, held, factor, tail = call(
        lambda *refs: prepare_kernel(spacing, steps, slots, *refs),
        "spread_queries",
        (
            pltpu.VMEM((per_source, rows, key_dim), BF16),
            pltpu.VMEM(states.shape, BF16),
            pltpu.VMEM((per_source, rows, 128), F32),
            pltpu.VMEM((per_source, steps, TAIL), F32),
        ),
        [ANY, ANY, SMEM, ANY, ANY],
        (VMEM,) * 4,
        [
            pltpu.VMEM(q.shape, BF16),
            pltpu.SMEM(dest_slot.shape, jnp.int32),
            pltpu.SMEM(arrive_step.shape, jnp.int32),
            pltpu.SemaphoreType.DMA((3 + per_source,)),
        ],
    )(in_hbm(dest_slot), in_hbm(arrive_step), decay, in_hbm(q), in_hbm(states))
    q_all = lax.all_to_all(spread, "rows", 0, 0, axis_index_groups=groups, tiled=True)
    readouts = call(
        lambda *refs: source_kernel(spacing, steps, slots, *refs),
        "source_readout",
        shape((per_source, steps, val_dim + TAIL), BF16),
        [VMEM] * 4,
        VMEM,
        cost=pl.CostEstimate(flops=2 * rows * states.size, bytes_accessed=32 << 20, transcendentals=0),
    )(q_all, held, factor, tail)
    back = lax.all_to_all(readouts, "rows", 0, 0, axis_index_groups=groups, tiled=True)
    heads = lax.axis_size("heads")
    columns = out_weight.shape[1] // heads
    partial = call(
        lambda *refs: row_kernel(steps, slots, *refs),
        "combine_project",
        shape((heads, rows, columns), BF16),
        [SMEM] + [VMEM] * 7,
        VMEM,
    )(
        decay, back, q, keys.reshape(rows, key_dim), values.reshape(rows, val_dim),
        gates.reshape(rows, val_dim), norm_gain.reshape(1, val_dim), out_weight,
    )
    shares = lax.all_to_all(partial, "heads", 0, 0, tiled=True)
    total = call(total_kernel, "sum_heads", shape((rows, columns), BF16), [VMEM], VMEM)(shares)
    return total.reshape(steps, slots, columns)


def solution(mesh):
    placed = (
        P(None, "rows", "heads"),
        P(None, "rows", "heads"),
        P(None, "rows", "heads"),
        P(None, "rows", "heads"),
        P("rows", "heads", None, None),
        P("rows"),
        P("rows"),
        P("heads"),
        P("heads"),
        P("heads", None),
    )
    return jax.shard_map(
        shards, mesh=mesh, in_specs=placed, out_specs=P(None, "rows", "heads"), check_vma=False
    )
```

time: 65.9 us -> 62.5 us (0.948)
  blocking collectives: 35.5 us -> 57.8 us
  waiting for transfers between devices: 13.6 us -> 0 us
  starting transfers between devices: 8.38 us -> 0 us
  local copies, waits for them, and re-layouts: 4.54 us -> 0.04 us
  Pallas kernels: 2.15 us -> 3.7 us
    all_to_all x0 -> x1, blocking collectives: none -> 22.5 us  [shards(): lax.all_to_all(spread, 'rows', 0, 0, axis_index_groups=groups, tiled=True)]
    all_to_all x1 -> x0, waiting for transfers between devices: 13.6 us -> none  [shards(): lax.all_to_all(jnp.broadcast_to(q[None], (per_source, rows, key_dim)), 'r...]
    all_to_all x1 -> x0, starting transfers between devices: 8.38 us -> none  [shards(): lax.all_to_all(jnp.broadcast_to(q[None], (per_source, rows, key_dim)), 'r...]
    unnamed x18 -> x12, local copies, waits for them, and re-layouts: 2.93 us -> 0.04 us
    broadcast_in_dim x1 -> x0, local copies, waits for them, and re-layouts: 1.62 us -> none  [shards(): jnp.broadcast_to(q[None], (per_source, rows, key_dim))]
    pallas_call x2 -> x4, Pallas kernels: 2.15 us -> 3.7 us  [the longest x1 1.62 us: shards(): call(lambda *refs: prepare_kernel(spacing, steps, slots, *refs), 'spread_...]
  transfers between devices with their start and end apart: 1 -> 0, of which waited for: 1 -> 0; matrix products, arithmetic and copies ran while one was open for 0% -> 0% of each run, Pallas kernels for 0% -> 0%
where the time goes in v2:
time: 62.5 us; the launch traced here: 62.3 us
  blocking collectives  57.8 us (92%)
  Pallas kernels  3.7 us (6%)
  between operations  0.75 us (1%)
    all_to_all x1, blocking collectives, shards(): shares = lax.all_to_all(partial, 'heads', 0, 0, tiled=True)  23.7 us
    all_to_all x1, blocking collectives, shards(): lax.all_to_all(spread, 'rows', 0, 0, axis_index_groups=groups, tiled=True)  22.5 us
    all_to_all x1, blocking collectives, shards(): lax.all_to_all(readouts, 'rows', 0, 0, axis_index_groups=groups, tiled=True)  11.6 us
    pallas_call x1, Pallas kernels, shards(): call(lambda *refs: prepare_kernel(spacing, steps, slots, *refs), 'spread_...  1.62 us

profile of v2, /device:TPU:9, one launch (start us, length us, event | category | flops | bytes accessed | tf_op | source)
XLA Modules:
  0.0 62.3 jit_solution(6988824133028694623)
XLA Ops:
  0.7 1.6 %spread_queries.1 = (bf16[8,64,256]{2,1,0:T(8,128)(2,1)S(1)}, bf16[8,256,512]{2,1,0:T(8,128)(2,1)S(1)}, f32[8,64,128]{2,1,0:T(8,128)S(1)}, f32[8,8,128]{2,1,0:T(8,128)S(1)}) custom-call(s32[8]{0:T(128)} %refs_0_.2, s32[8]{0:T(128)} %refs_1_.1, f32[1]{0:T(128)S(6)} %copy.11.refs_2_.refs_0_, bf16[64,256]{1,0:T(8,128)(2,1)} %bitcast.7, ...), custom_call_target="tpu_custom_call" | custom-call | tf_op jit(solution)/shard_map/spread_queries/pallas_call | solution.py:148
  2.3 0.0 copy-start
  2.3 0.0 copy-start.1
  2.3 0.0 copy-start.2
  2.3 0.0 copy-start.3
  2.3 0.0 copy-start.4
  2.3 0.0 copy-start.5
  2.4 22.5 %all_to_all.15.refs_0_ = bf16[8,64,256]{2,1,0:T(8,128)(2,1)S(1)} all-to-all(bf16[8,64,256]{2,1,0:T(8,128)(2,1)S(1)} %get-tuple-element.9), channel_id=1, replica_groups={{0,64,128,192,256,320,384,448},{16,80,144,208,272,336,400,464},{32,96,1..., dimensions={0} | all-to-all | bytes 524288 | tf_op jit(solution)/shard_map/all_to_all | solution.py:166
  24.9 0.5 source_readout.1
  25.4 11.6 %all_to_all.16.refs_1_ = bf16[8,8,640]{2,1,0:T(8,128)(2,1)S(1)} all-to-all(bf16[8,8,640]{2,1,0:T(8,128)(2,1)S(1)} %source_readout.1), channel_id=1, replica_groups={{0,64,128,192,256,320,384,448},{16,80,144,208,272,336,400,464},{32,96,1..., dimensions={0} | all-to-all | bytes 163840 | tf_op jit(solution)/shard_map/all_to_all | solution.py:175
  37.0 0.0 copy-done
  37.0 0.0 copy-done.1
  37.0 0.0 copy-done.2
  37.0 0.0 copy-done.3
  37.0 0.0 copy-done.4
  37.0 0.0 copy-done.5
  37.0 0.9 %combine_project.1 = bf16[16,64,128]{2,1,0:T(8,128)(2,1)S(1)} custom-call(f32[1]{0:T(128)S(6)} %copy.11.refs_2_.refs_0_, bf16[8,8,640]{2,1,0:T(8,128)(2,1)S(1)} %all_to_all.16.refs_1_, bf16[64,256]{1,0:T(8,128)(2,1)S(1)} %bitcast.8, bf16[64,256]{1,0:T(8,128)(2,1)S(1)} %bitcast.11, bf16[64,512]{1,0:T(8,128)(2,1)S(1)} %bitcast.9, ...), custom_call_target="tpu_custom_call" | custom-call | tf_op jit(solution)/shard_map/combine_project/pallas_call | solution.py:178
  37.9 23.7 %all_to_all.17.shares_ref = bf16[16,64,128]{2,1,0:T(8,128)(2,1)S(1)} all-to-all(bf16[16,64,128]{2,1,0:T(8,128)(2,1)S(1)} %combine_project.1), channel_id=1, replica_groups=mesh['rows'=32,'heads'=16] {'heads'}, dimensions={0} | all-to-all | bytes 524288 | tf_op jit(solution)/shard_map/all_to_all | solution.py:188
  61.6 0.6 %sum_heads.1 = bf16[64,128]{1,0:T(8,128)(2,1)} custom-call(bf16[16,64,128]{2,1,0:T(8,128)(2,1)S(1)} %all_to_all.17.shares_ref), custom_call_target="tpu_custom_call" | custom-call | tf_op jit(solution)/shard_map/sum_heads/pallas_call | solution.py:189
Async XLA Ops:
  2.3 34.7 %copy-start = (bf16[512,2048]{1,0:T(8,128)(2,1)S(1)}, bf16[512,2048]{1,0:T(8,128)(2,1)}, u32[]{:S(2)}) copy-start(bf16[512,2048]{1,0:T(8,128)(2,1)} %refs_7_.1) | copy-start | bytes 6291460
  2.3 34.7 %copy-start.1 = (bf16[8,8,256]{2,1,0:T(8,128)(2,1)S(1)}, bf16[8,8,256]{2,1,0:T(8,128)(2,1)}, u32[]{:S(2)}) copy-start(bf16[8,8,256]{2,1,0:T(8,128)(2,1)} %param.10) | copy-start | bytes 98308
  2.3 34.7 %copy-start.2 = (bf16[8,8,512]{2,1,0:T(8,128)(2,1)S(1)}, bf16[8,8,512]{2,1,0:T(8,128)(2,1)}, u32[]{:S(2)}) copy-start(bf16[8,8,512]{2,1,0:T(8,128)(2,1)} %param.12) | copy-start | bytes 196612
  2.3 34.7 %copy-start.3 = (bf16[8,8,512]{2,1,0:T(8,128)(2,1)S(1)}, bf16[8,8,512]{2,1,0:T(8,128)(2,1)}, u32[]{:S(2)}) copy-start(bf16[8,8,512]{2,1,0:T(8,128)(2,1)} %param.13) | copy-start | bytes 196612
  2.3 34.7 %copy-start.4 = (bf16[8,8,256]{2,1,0:T(8,128)(2,1)S(1)}, bf16[8,8,256]{2,1,0:T(8,128)(2,1)}, u32[]{:S(2)}) copy-start(bf16[8,8,256]{2,1,0:T(8,128)(2,1)} %param.11) | copy-start | bytes 98308
  2.3 34.7 %copy-start.5 = (f32[512]{0:T(512)S(1)}, f32[512]{0:T(512)}, u32[]{:S(2)}) copy-start(f32[512]{0:T(512)} %param.18) | copy-start | bytes 6148

commit v3 on v2

--- a/solution.py
+++ b/solution.py
@@ -11,6 +11,9 @@
 SMEM = pl.BlockSpec(memory_space=pltpu.SMEM)
 ANY = pl.BlockSpec(memory_space=pl.ANY)
 TAIL = 128
+SOURCE_ORDER = (5, 7, 1, 3, 4, 6, 0, 2)
+RETURN_ORDER = (5, 6, 7, 0, 1, 2, 3, 4)
+HEAD_ORDER = tuple(range(15, -1, -1))
 
 
 def in_hbm(value):
@@ -26,9 +29,9 @@
 
 def prepare_kernel(
     spacing, steps, slots, dest_in, step_in, decay_ref, q_in, state_in,
-    spread_ref, state_ref, factor_ref, tail_ref, q_ref, dest_ref, step_ref, sems,
+    spread_ref, state_ref, scale_ref, pick_ref, tail_ref, q_ref, dest_ref, step_ref, sems,
 ):
-    peers = factor_ref.shape[0]
+    peers = scale_ref.shape[0]
     first = pltpu.make_async_copy(q_in, q_ref, sems.at[0])
     ints = [
         pltpu.make_async_copy(dest_in, dest_ref, sems.at[1]),
@@ -46,33 +49,34 @@
         copy.wait()
     member = lax.div(lax.axis_index("rows"), spacing)
     decay = decay_ref[0]
-    row = lax.broadcasted_iota(jnp.int32, (steps * slots, 128), 0)
+    line = lax.broadcasted_iota(jnp.int32, (steps, 128), 0)
+    place = lax.broadcasted_iota(jnp.int32, (slots, 128), 0)
     lane = lax.broadcasted_iota(jnp.int32, (steps, TAIL), 1)
     for order in range(peers):
         slot = lax.rem(dest_ref[order], slots)
         joined = step_ref[order]
-        age = lax.div(row, slots) - joined + 1
-        mine = (lax.rem(row, slots) == slot) & (age > 0)
+        age = line - joined + 1
         peer = lax.rem(member + order, peers)
-        factor_ref[peer] = jnp.where(mine, int_power(decay, age, steps), 0.0)
+        scale_ref[peer] = jnp.where(age > 0, int_power(decay, age, steps), 0.0)
+        pick_ref[peer] = jnp.where(place == slot, 1.0, 0.0)
         tail_ref[peer] = jnp.where(lane < TAIL // 2, slot, joined).astype(F32)
     for copy in copies[3:]:
         copy.wait()
 
 
-def source_kernel(spacing, steps, slots, q_ref, state_ref, factor_ref, tail_ref, out_ref):
+def source_kernel(spacing, steps, slots, q_ref, state_ref, scale_ref, pick_ref, tail_ref, out_ref):
     peers, _, width = state_ref.shape
     member = lax.div(lax.axis_index("rows"), spacing)
-    for peer in range(peers):
+    for block, peer in enumerate(SOURCE_ORDER):
         order = lax.rem(peer - member + peers, peers)
-        full = jnp.dot(q_ref[peer], state_ref[order], preferred_element_type=F32)
-        factor = factor_ref[peer]
+        full = jnp.dot(q_ref[block], state_ref[order], preferred_element_type=F32)
+        scale, pick = scale_ref[peer], pick_ref[peer][None]
         parts = []
         for col in range(0, width, 128):
-            part = full[:, col : col + 128] * factor
-            parts.append(jnp.sum(part.reshape(steps, slots, 128), axis=1))
+            part = full[:, col : col + 128].reshape(steps, slots, 128) * pick
+            parts.append(jnp.sum(part, axis=1) * scale)
         parts.append(tail_ref[peer])
-        out_ref[peer] = jnp.concatenate(parts, axis=1).astype(BF16)
+        out_ref[RETURN_ORDER.index(peer)] = jnp.concatenate(parts, axis=1).astype(BF16)
 
 
 def row_kernel(steps, slots, decay_ref, back_ref, q_ref, k_ref, v_ref, g_ref, gain_ref, w_ref, out_ref):
@@ -112,7 +116,7 @@
     shares, _, columns = out_ref.shape
     for share in range(shares):
         part = jnp.dot(normed, w_ref[:, share * columns : (share + 1) * columns], preferred_element_type=F32)
-        out_ref[share] = part.astype(out_ref.dtype)
+        out_ref[HEAD_ORDER.index(share)] = part.astype(out_ref.dtype)
 
 
 def total_kernel(shares_ref, out_ref):
@@ -141,21 +145,25 @@
     rows = steps * slots
     per_source = dest_slot.shape[0]
     spacing = lax.axis_size("rows") // per_source
-    groups = [[first + spacing * m for m in range(per_source)] for first in range(spacing)]
+    sources, returns = [
+        [[first + spacing * member for member in order] for first in range(spacing)]
+        for order in (SOURCE_ORDER, RETURN_ORDER)
+    ]
     shape = jax.ShapeDtypeStruct
     q = queries.reshape(rows, key_dim)
     states = prefill_states.reshape(per_source, key_dim, val_dim)
-    spread, held, factor, tail = call(
+    spread, held, scale, pick, tail = call(
         lambda *refs: prepare_kernel(spacing, steps, slots, *refs),
         "spread_queries",
         (
             pltpu.VMEM((per_source, rows, key_dim), BF16),
             pltpu.VMEM(states.shape, BF16),
-            pltpu.VMEM((per_source, rows, 128), F32),
+            pltpu.VMEM((per_source, steps, 128), F32),
+            pltpu.VMEM((per_source, slots, 128), F32),
             pltpu.VMEM((per_source, steps, TAIL), F32),
         ),
         [ANY, ANY, SMEM, ANY, ANY],
-        (VMEM,) * 4,
+        (VMEM,) * 5,
         [
             pltpu.VMEM(q.shape, BF16),
             pltpu.SMEM(dest_slot.shape, jnp.int32),
@@ -163,16 +171,16 @@
             pltpu.SemaphoreType.DMA((3 + per_source,)),
         ],
     )(in_hbm(dest_slot), in_hbm(arrive_step), decay, in_hbm(q), in_hbm(states))
-    q_all = lax.all_to_all(spread, "rows", 0, 0, axis_index_groups=groups, tiled=True)
+    q_all = lax.all_to_all(spread, "rows", 0, 0, axis_index_groups=sources, tiled=True)
     readouts = call(
         lambda *refs: source_kernel(spacing, steps, slots, *refs),
         "source_readout",
         shape((per_source, steps, val_dim + TAIL), BF16),
-        [VMEM] * 4,
+        [VMEM] * 5,
         VMEM,
         cost=pl.CostEstimate(flops=2 * rows * states.size, bytes_accessed=32 << 20, transcendentals=0),
-    )(q_all, held, factor, tail)
-    back = lax.all_to_all(readouts, "rows", 0, 0, axis_index_groups=groups, tiled=True)
+    )(q_all, held, scale, pick, tail)
+    back = lax.all_to_all(readouts, "rows", 0, 0, axis_index_groups=returns, tiled=True)
     heads = lax.axis_size("heads")
     columns = out_weight.shape[1] // heads
     partial = call(
@@ -185,7 +193,7 @@
         decay, back, q, keys.reshape(rows, key_dim), values.reshape(rows, val_dim),
         gates.reshape(rows, val_dim), norm_gain.reshape(1, val_dim), out_weight,
     )
-    shares = lax.all_to_all(partial, "heads", 0, 0, tiled=True)
+    shares = lax.all_to_all(partial, "heads", 0, 0, axis_index_groups=[list(HEAD_ORDER)], tiled=True)
     total = call(total_kernel, "sum_heads", shape((rows, columns), BF16), [VMEM], VMEM)(shares)
     return total.reshape(steps, slots, columns)
 

time: 62.5 us -> 54.2 us (0.87)
  the two profiles are of different devices: /device:TPU:9 before, /device:TPU:49 now
where the time goes in v3:
time: 54.2 us; the launch traced here: 54 us
  blocking collectives  49.5 us (91%)
  Pallas kernels  3.71 us (7%)
  between operations  0.75 us (1%)
    all_to_all x1, blocking collectives, shards(): lax.all_to_all(partial, 'heads', 0, 0, axis_index_groups=[list(HEAD_ORDER...  22.6 us
    all_to_all x1, blocking collectives, shards(): lax.all_to_all(spread, 'rows', 0, 0, axis_index_groups=sources, tiled=True)  16.1 us
    all_to_all x1, blocking collectives, shards(): lax.all_to_all(readouts, 'rows', 0, 0, axis_index_groups=returns, tiled=T...  10.7 us
    pallas_call x1, Pallas kernels, shards(): call(lambda *refs: prepare_kernel(spacing, steps, slots, *refs), 'spread_...  1.62 us

profile of v3, /device:TPU:49, one launch (start us, length us, event | category | flops | bytes accessed | tf_op | source)
XLA Modules:
  0.0 54.0 jit_solution(179417981439671969)
XLA Ops:
  0.7 1.6 %spread_queries.1 = (bf16[8,64,256]{2,1,0:T(8,128)(2,1)S(1)}, bf16[8,256,512]{2,1,0:T(8,128)(2,1)S(1)}, f32[8,8,128]{2,1,0:T(8,128)S(1)}, f32[8,8,128]{2,1,0:T(8,128)S(1)}, f32[8,8,128]{2,1,0:T(8,128)S(1)}) custom-call(s32[8]{0:T(128)} %refs_0_.2, s32[8]{0:T(128)} %refs_1_.1, f32[1]{0:T(128)S(6)} %copy.11.refs_2_.refs_0_, bf16[64,256]{1,0:T(8,128)(2,1)} %bitcast.7, ...), custom_call_target="tpu_custom_call" | custom-call | tf_op jit(solution)/shard_map/spread_queries/pallas_call | solution.py:155
  2.3 0.0 copy-start
  2.3 0.0 copy-start.1
  2.3 0.0 copy-start.2
  2.3 0.0 copy-start.3
  2.3 0.0 copy-start.4
  2.3 0.0 copy-start.5
  2.4 16.1 %all_to_all.15.refs_0_ = bf16[8,64,256]{2,1,0:T(8,128)(2,1)S(1)} all-to-all(bf16[8,64,256]{2,1,0:T(8,128)(2,1)S(1)} %get-tuple-element.10), channel_id=1, replica_groups={{320,448,64,192,256,384,0,128},{336,464,80,208,272,400,16,144},{352,480..., dimensions={0} | all-to-all | bytes 524288 | tf_op jit(solution)/shard_map/all_to_all | solution.py:174
  18.5 0.5 source_readout.1
  19.0 10.7 %all_to_all.16.refs_1_ = bf16[8,8,640]{2,1,0:T(8,128)(2,1)S(1)} all-to-all(bf16[8,8,640]{2,1,0:T(8,128)(2,1)S(1)} %source_readout.1), channel_id=1, replica_groups={{320,384,448,0,64,128,192,256},{336,400,464,16,80,144,208,272},{352,416..., dimensions={0} | all-to-all | bytes 163840 | tf_op jit(solution)/shard_map/all_to_all | solution.py:183
  29.8 0.0 copy-done
  29.8 0.0 copy-done.1
  29.8 0.0 copy-done.2
  29.8 0.0 copy-done.3
  29.8 0.0 copy-done.4
  29.8 0.0 copy-done.5
  29.8 0.9 %combine_project.1 = bf16[16,64,128]{2,1,0:T(8,128)(2,1)S(1)} custom-call(f32[1]{0:T(128)S(6)} %copy.11.refs_2_.refs_0_, bf16[8,8,640]{2,1,0:T(8,128)(2,1)S(1)} %all_to_all.16.refs_1_, bf16[64,256]{1,0:T(8,128)(2,1)S(1)} %bitcast.8, bf16[64,256]{1,0:T(8,128)(2,1)S(1)} %bitcast.11, bf16[64,512]{1,0:T(8,128)(2,1)S(1)} %bitcast.9, ...), custom_call_target="tpu_custom_call" | custom-call | tf_op jit(solution)/shard_map/combine_project/pallas_call | solution.py:186
  30.7 22.6 %all_to_all.17.shares_ref = bf16[16,64,128]{2,1,0:T(8,128)(2,1)S(1)} all-to-all(bf16[16,64,128]{2,1,0:T(8,128)(2,1)S(1)} %combine_project.1), channel_id=1, replica_groups={{15,14,13,12,11,10,9,8,7,6,5,4,3,2,1,0},{31,30,29,28,27,26,25,24,23,22,..., dimensions={0} | all-to-all | bytes 524288 | tf_op jit(solution)/shard_map/all_to_all | solution.py:196
  53.3 0.6 %sum_heads.1 = bf16[64,128]{1,0:T(8,128)(2,1)} custom-call(bf16[16,64,128]{2,1,0:T(8,128)(2,1)S(1)} %all_to_all.17.shares_ref), custom_call_target="tpu_custom_call" | custom-call | tf_op jit(solution)/shard_map/sum_heads/pallas_call | solution.py:197
Async XLA Ops:
  2.3 27.5 %copy-start = (bf16[512,2048]{1,0:T(8,128)(2,1)S(1)}, bf16[512,2048]{1,0:T(8,128)(2,1)}, u32[]{:S(2)}) copy-start(bf16[512,2048]{1,0:T(8,128)(2,1)} %refs_7_.1) | copy-start | bytes 6291460
  2.3 27.5 %copy-start.1 = (bf16[8,8,256]{2,1,0:T(8,128)(2,1)S(1)}, bf16[8,8,256]{2,1,0:T(8,128)(2,1)}, u32[]{:S(2)}) copy-start(bf16[8,8,256]{2,1,0:T(8,128)(2,1)} %param.10) | copy-start | bytes 98308
  2.3 27.5 %copy-start.2 = (bf16[8,8,512]{2,1,0:T(8,128)(2,1)S(1)}, bf16[8,8,512]{2,1,0:T(8,128)(2,1)}, u32[]{:S(2)}) copy-start(bf16[8,8,512]{2,1,0:T(8,128)(2,1)} %param.12) | copy-start | bytes 196612
  2.3 27.5 %copy-start.3 = (bf16[8,8,512]{2,1,0:T(8,128)(2,1)S(1)}, bf16[8,8,512]{2,1,0:T(8,128)(2,1)}, u32[]{:S(2)}) copy-start(bf16[8,8,512]{2,1,0:T(8,128)(2,1)} %param.13) | copy-start | bytes 196612
  2.3 27.5 %copy-start.4 = (bf16[8,8,256]{2,1,0:T(8,128)(2,1)S(1)}, bf16[8,8,256]{2,1,0:T(8,128)(2,1)}, u32[]{:S(2)}) copy-start(bf16[8,8,256]{2,1,0:T(8,128)(2,1)} %param.11) | copy-start | bytes 98308
  2.3 27.5 %copy-start.5 = (f32[512]{0:T(512)S(1)}, f32[512]{0:T(512)}, u32[]{:S(2)}) copy-start(f32[512]{0:T(512)} %param.18) | copy-start | bytes 6148

commit v4 on v3

--- a/solution.py
+++ b/solution.py
@@ -13,7 +13,7 @@
 TAIL = 128
 SOURCE_ORDER = (5, 7, 1, 3, 4, 6, 0, 2)
 RETURN_ORDER = (5, 6, 7, 0, 1, 2, 3, 4)
-HEAD_ORDER = tuple(range(15, -1, -1))
+HEAD_ORDER = (15, 13, 14) + tuple(range(12, -1, -1))
 
 
 def in_hbm(value):
@@ -28,8 +28,8 @@
 
 
 def prepare_kernel(
-    spacing, steps, slots, dest_in, step_in, decay_ref, q_in, state_in,
-    spread_ref, state_ref, scale_ref, pick_ref, tail_ref, q_ref, dest_ref, step_ref, sems,
+    spacing, steps, slots, dest_in, step_in, decay_ref, q_in,
+    spread_ref, scale_ref, pick_ref, tail_ref, q_ref, dest_ref, step_ref, sems,
 ):
     peers = scale_ref.shape[0]
     first = pltpu.make_async_copy(q_in, q_ref, sems.at[0])
@@ -37,10 +37,7 @@
         pltpu.make_async_copy(dest_in, dest_ref, sems.at[1]),
         pltpu.make_async_copy(step_in, step_ref, sems.at[2]),
     ]
-    copies = [first] + ints + [
-        pltpu.make_async_copy(state_in.at[order], state_ref.at[order], sems.at[3 + order]) for order in range(peers)
-    ]
-    for copy in copies:
+    for copy in [first] + ints:
         copy.start()
     first.wait()
     for peer in range(peers):
@@ -60,8 +57,6 @@
         scale_ref[peer] = jnp.where(age > 0, int_power(decay, age, steps), 0.0)
         pick_ref[peer] = jnp.where(place == slot, 1.0, 0.0)
         tail_ref[peer] = jnp.where(lane < TAIL // 2, slot, joined).astype(F32)
-    for copy in copies[3:]:
-        copy.wait()
 
 
 def source_kernel(spacing, steps, slots, q_ref, state_ref, scale_ref, pick_ref, tail_ref, out_ref):
@@ -150,27 +145,28 @@
         for order in (SOURCE_ORDER, RETURN_ORDER)
     ]
     shape = jax.ShapeDtypeStruct
+    spread_size = per_source * rows * key_dim
     q = queries.reshape(rows, key_dim)
     states = prefill_states.reshape(per_source, key_dim, val_dim)
-    spread, held, scale, pick, tail = call(
+    spread, scale, pick, tail = call(
         lambda *refs: prepare_kernel(spacing, steps, slots, *refs),
         "spread_queries",
         (
             pltpu.VMEM((per_source, rows, key_dim), BF16),
-            pltpu.VMEM(states.shape, BF16),
             pltpu.VMEM((per_source, steps, 128), F32),
             pltpu.VMEM((per_source, slots, 128), F32),
             pltpu.VMEM((per_source, steps, TAIL), F32),
         ),
-        [ANY, ANY, SMEM, ANY, ANY],
-        (VMEM,) * 5,
+        [ANY, ANY, SMEM, ANY],
+        (VMEM,) * 4,
         [
             pltpu.VMEM(q.shape, BF16),
             pltpu.SMEM(dest_slot.shape, jnp.int32),
             pltpu.SMEM(arrive_step.shape, jnp.int32),
-            pltpu.SemaphoreType.DMA((3 + per_source,)),
+            pltpu.SemaphoreType.DMA((3,)),
         ],
-    )(in_hbm(dest_slot), in_hbm(arrive_step), decay, in_hbm(q), in_hbm(states))
+        pl.CostEstimate(flops=20 * 10**9, bytes_accessed=2 * spread_size, transcendentals=0),
+    )(in_hbm(dest_slot), in_hbm(arrive_step), decay, in_hbm(q))
     q_all = lax.all_to_all(spread, "rows", 0, 0, axis_index_groups=sources, tiled=True)
     readouts = call(
         lambda *refs: source_kernel(spacing, steps, slots, *refs),
@@ -178,8 +174,8 @@
         shape((per_source, steps, val_dim + TAIL), BF16),
         [VMEM] * 5,
         VMEM,
-        cost=pl.CostEstimate(flops=2 * rows * states.size, bytes_accessed=32 << 20, transcendentals=0),
-    )(q_all, held, scale, pick, tail)
+        cost=pl.CostEstimate(flops=20 * 10**9, bytes_accessed=2 * states.size, transcendentals=0),
+    )(q_all, states, scale, pick, tail)
     back = lax.all_to_all(readouts, "rows", 0, 0, axis_index_groups=returns, tiled=True)
     heads = lax.axis_size("heads")
     columns = out_weight.shape[1] // heads

time: 54.2 us -> 53.5 us (0.987)
  Pallas kernels: 3.71 us -> 3.14 us
    pallas_call x1, Pallas kernels: 1.62 us -> 1.03 us  [shards(): call(lambda *refs: prepare_kernel(spacing, steps, slots, *refs), 'spread_...]
where the time goes in v4:
time: 53.5 us; the launch traced here: 53.3 us
  blocking collectives  49.3 us (92%)
  Pallas kernels  3.14 us (6%)
  between operations  0.74 us (1%)
    all_to_all x1, blocking collectives, shards(): lax.all_to_all(partial, 'heads', 0, 0, axis_index_groups=[list(HEAD_ORDER...  22.5 us
    all_to_all x1, blocking collectives, shards(): lax.all_to_all(spread, 'rows', 0, 0, axis_index_groups=sources, tiled=True)  16 us
    all_to_all x1, blocking collectives, shards(): lax.all_to_all(readouts, 'rows', 0, 0, axis_index_groups=returns, tiled=T...  10.9 us

profile of v4, /device:TPU:49, one launch (start us, length us, event | category | flops | bytes accessed | tf_op | source)
XLA Modules:
  0.0 53.3 jit_solution(1423158535930810995)
XLA Ops:
  0.7 0.0 copy-start.6
  0.7 1.0 %spread_queries.1 = (bf16[8,64,256]{2,1,0:T(8,128)(2,1)S(1)}, f32[8,8,128]{2,1,0:T(8,128)S(1)}, f32[8,8,128]{2,1,0:T(8,128)S(1)}, f32[8,8,128]{2,1,0:T(8,128)S(1)}) custom-call(s32[8]{0:T(128)} %refs_0_.2, s32[8]{0:T(128)} %refs_1_.1, f32[1]{0:T(128)S(6)} %copy.11.refs_2_.refs_0_, bf16[64,256]{1,0:T(8,128)(2,1)} %bitcast.9), custom_call_target="tpu_custom_call" | custom-call | flops 20000000000 | bytes 262144 | tf_op jit(solution)/shard_map/spread_queries/pallas_call | solution.py:151
  1.7 16.0 %all_to_all.15.refs_0_ = bf16[8,64,256]{2,1,0:T(8,128)(2,1)S(1)} all-to-all(bf16[8,64,256]{2,1,0:T(8,128)(2,1)S(1)} %get-tuple-element.9), channel_id=1, replica_groups={{320,448,64,192,256,384,0,128},{336,464,80,208,272,400,16,144},{352,480..., dimensions={0} | all-to-all | bytes 524288 | tf_op jit(solution)/shard_map/all_to_all | solution.py:170
  17.7 0.0 copy-done.6
  17.7 0.0 copy-start
  17.7 0.0 copy-start.1
  17.7 0.0 copy-start.2
  17.7 0.0 copy-start.3
  17.7 0.0 copy-start.4
  17.7 0.0 copy-start.5
  17.8 0.5 %source_readout.1 = bf16[8,8,640]{2,1,0:T(8,128)(2,1)S(1)} custom-call(bf16[8,64,256]{2,1,0:T(8,128)(2,1)S(1)} %all_to_all.15.refs_0_, bf16[8,256,512]{2,1,0:T(8,128)(2,1)S(1)} %bitcast.13, f32[8,8,128]{2,1,0:T(8,128)S(1)} %get-tuple-element.10.refs_2_, f32[8,8,128]{2,1,0:T(8,128)S(1)} %get-tuple-element.11.refs_3_, f32[8,8,128]{2,1,0:T(8,128)S(1)} %get-tuple-element.12.refs_4_), custom_call_target="tpu_custom_call" | custom-call | flops 20000000000 | bytes 2097152 | tf_op jit(solution)/shard_map/source_readout/pallas_call | solution.py:171
  18.3 10.9 %all_to_all.16.refs_1_ = bf16[8,8,640]{2,1,0:T(8,128)(2,1)S(1)} all-to-all(bf16[8,8,640]{2,1,0:T(8,128)(2,1)S(1)} %source_readout.1), channel_id=1, replica_groups={{320,384,448,0,64,128,192,256},{336,400,464,16,80,144,208,272},{352,416..., dimensions={0} | all-to-all | bytes 163840 | tf_op jit(solution)/shard_map/all_to_all | solution.py:179
  29.2 0.0 copy-done
  29.2 0.0 copy-done.1
  29.2 0.0 copy-done.2
  29.2 0.0 copy-done.3
  29.2 0.0 copy-done.4
  29.2 0.0 copy-done.5
  29.2 0.9 %combine_project.1 = bf16[16,64,128]{2,1,0:T(8,128)(2,1)S(1)} custom-call(f32[1]{0:T(128)S(6)} %copy.11.refs_2_.refs_0_, bf16[8,8,640]{2,1,0:T(8,128)(2,1)S(1)} %all_to_all.16.refs_1_, bf16[64,256]{1,0:T(8,128)(2,1)S(1)} %bitcast.10, bf16[64,256]{1,0:T(8,128)(2,1)S(1)} %bitcast.11, bf16[64,512]{1,0:T(8,128)(2,1)S(1)} %bitcast.7, ...), custom_call_target="tpu_custom_call" | custom-call | tf_op jit(solution)/shard_map/combine_project/pallas_call | solution.py:182
  30.1 22.5 %all_to_all.17.shares_ref = bf16[16,64,128]{2,1,0:T(8,128)(2,1)S(1)} all-to-all(bf16[16,64,128]{2,1,0:T(8,128)(2,1)S(1)} %combine_project.1), channel_id=1, replica_groups={{15,13,14,12,11,10,9,8,7,6,5,4,3,2,1,0},{31,29,30,28,27,26,25,24,23,22,..., dimensions={0} | all-to-all | bytes 524288 | tf_op jit(solution)/shard_map/all_to_all | solution.py:192
  52.6 0.6 %sum_heads.1 = bf16[64,128]{1,0:T(8,128)(2,1)} custom-call(bf16[16,64,128]{2,1,0:T(8,128)(2,1)S(1)} %all_to_all.17.shares_ref), custom_call_target="tpu_custom_call" | custom-call | tf_op jit(solution)/shard_map/sum_heads/pallas_call | solution.py:193
Async XLA Ops:
  0.7 17.1 %copy-start.6 = (bf16[8,1,256,512]{3,2,1,0:T(8,128)(2,1)S(1)}, bf16[8,1,256,512]{3,2,1,0:T(8,128)(2,1)}, u32[]{:S(2)}) copy-start(bf16[8,1,256,512]{3,2,1,0:T(8,128)(2,1)} %param.14) | copy-start | bytes 6291460
  17.7 11.5 %copy-start = (bf16[512,2048]{1,0:T(8,128)(2,1)S(1)}, bf16[512,2048]{1,0:T(8,128)(2,1)}, u32[]{:S(2)}) copy-start(bf16[512,2048]{1,0:T(8,128)(2,1)} %refs_7_.1) | copy-start | bytes 6291460
  17.7 11.5 %copy-start.1 = (bf16[8,8,512]{2,1,0:T(8,128)(2,1)S(1)}, bf16[8,8,512]{2,1,0:T(8,128)(2,1)}, u32[]{:S(2)}) copy-start(bf16[8,8,512]{2,1,0:T(8,128)(2,1)} %param.12) | copy-start | bytes 196612
  17.7 11.5 %copy-start.2 = (bf16[8,8,512]{2,1,0:T(8,128)(2,1)S(1)}, bf16[8,8,512]{2,1,0:T(8,128)(2,1)}, u32[]{:S(2)}) copy-start(bf16[8,8,512]{2,1,0:T(8,128)(2,1)} %param.13) | copy-start | bytes 196612
  17.7 11.5 %copy-start.3 = (bf16[8,8,256]{2,1,0:T(8,128)(2,1)S(1)}, bf16[8,8,256]{2,1,0:T(8,128)(2,1)}, u32[]{:S(2)}) copy-start(bf16[8,8,256]{2,1,0:T(8,128)(2,1)} %param.10) | copy-start | bytes 98308
  17.7 11.5 %copy-start.4 = (bf16[8,8,256]{2,1,0:T(8,128)(2,1)S(1)}, bf16[8,8,256]{2,1,0:T(8,128)(2,1)}, u32[]{:S(2)}) copy-start(bf16[8,8,256]{2,1,0:T(8,128)(2,1)} %param.11) | copy-start | bytes 98308
  17.7 11.5 %copy-start.5 = (f32[512]{0:T(512)S(1)}, f32[512]{0:T(512)}, u32[]{:S(2)}) copy-start(f32[512]{0:T(512)} %param.18) | copy-start | bytes 6148

commit v5 on v4

--- a/solution.py
+++ b/solution.py
@@ -13,7 +13,7 @@
 TAIL = 128
 SOURCE_ORDER = (5, 7, 1, 3, 4, 6, 0, 2)
 RETURN_ORDER = (5, 6, 7, 0, 1, 2, 3, 4)
-HEAD_ORDER = (15, 13, 14) + tuple(range(12, -1, -1))
+HEAD_ORDER = (15, 13, 14, 10, 12, 8, 11, 6, 9, 4, 7, 2, 5, 1, 3, 0)
 
 
 def in_hbm(value):

time: 53.5 us -> 53 us (level)
  no operation moved by 1% of the time
where the time goes in v5:
time: 53 us; the launch traced here: 52.8 us
  blocking collectives  48.8 us (92%)
  Pallas kernels  3.14 us (6%)
  between operations  0.74 us (1%)
    all_to_all x1, blocking collectives, shards(): lax.all_to_all(partial, 'heads', 0, 0, axis_index_groups=[list(HEAD_ORDER...  22 us
    all_to_all x1, blocking collectives, shards(): lax.all_to_all(spread, 'rows', 0, 0, axis_index_groups=sources, tiled=True)  16 us
    all_to_all x1, blocking collectives, shards(): lax.all_to_all(readouts, 'rows', 0, 0, axis_index_groups=returns, tiled=T...  10.9 us

profile of v5, /device:TPU:49, one launch (start us, length us, event | category | flops | bytes accessed | tf_op | source)
XLA Modules:
  0.0 52.8 jit_solution(11462009064810827733)
XLA Ops:
  0.7 0.0 copy-start.6
  0.7 1.0 %spread_queries.1 = (bf16[8,64,256]{2,1,0:T(8,128)(2,1)S(1)}, f32[8,8,128]{2,1,0:T(8,128)S(1)}, f32[8,8,128]{2,1,0:T(8,128)S(1)}, f32[8,8,128]{2,1,0:T(8,128)S(1)}) custom-call(s32[8]{0:T(128)} %refs_0_.2, s32[8]{0:T(128)} %refs_1_.1, f32[1]{0:T(128)S(6)} %copy.11.refs_2_.refs_0_, bf16[64,256]{1,0:T(8,128)(2,1)} %bitcast.9), custom_call_target="tpu_custom_call" | custom-call | flops 20000000000 | bytes 262144 | tf_op jit(solution)/shard_map/spread_queries/pallas_call | solution.py:151
  1.7 16.0 %all_to_all.15.refs_0_ = bf16[8,64,256]{2,1,0:T(8,128)(2,1)S(1)} all-to-all(bf16[8,64,256]{2,1,0:T(8,128)(2,1)S(1)} %get-tuple-element.9), channel_id=1, replica_groups={{320,448,64,192,256,384,0,128},{336,464,80,208,272,400,16,144},{352,480..., dimensions={0} | all-to-all | bytes 524288 | tf_op jit(solution)/shard_map/all_to_all | solution.py:170
  17.7 0.0 copy-done.6
  17.7 0.0 copy-start
  17.7 0.0 copy-start.1
  17.7 0.0 copy-start.2
  17.7 0.0 copy-start.3
  17.7 0.0 copy-start.4
  17.7 0.0 copy-start.5
  17.8 0.5 %source_readout.1 = bf16[8,8,640]{2,1,0:T(8,128)(2,1)S(1)} custom-call(bf16[8,64,256]{2,1,0:T(8,128)(2,1)S(1)} %all_to_all.15.refs_0_, bf16[8,256,512]{2,1,0:T(8,128)(2,1)S(1)} %bitcast.13, f32[8,8,128]{2,1,0:T(8,128)S(1)} %get-tuple-element.10.refs_2_, f32[8,8,128]{2,1,0:T(8,128)S(1)} %get-tuple-element.11.refs_3_, f32[8,8,128]{2,1,0:T(8,128)S(1)} %get-tuple-element.12.refs_4_), custom_call_target="tpu_custom_call" | custom-call | flops 20000000000 | bytes 2097152 | tf_op jit(solution)/shard_map/source_readout/pallas_call | solution.py:171
  18.3 10.9 %all_to_all.16.refs_1_ = bf16[8,8,640]{2,1,0:T(8,128)(2,1)S(1)} all-to-all(bf16[8,8,640]{2,1,0:T(8,128)(2,1)S(1)} %source_readout.1), channel_id=1, replica_groups={{320,384,448,0,64,128,192,256},{336,400,464,16,80,144,208,272},{352,416..., dimensions={0} | all-to-all | bytes 163840 | tf_op jit(solution)/shard_map/all_to_all | solution.py:179
  29.2 0.0 copy-done
  29.2 0.0 copy-done.1
  29.2 0.0 copy-done.2
  29.2 0.0 copy-done.3
  29.2 0.0 copy-done.4
  29.2 0.0 copy-done.5
  29.2 0.9 %combine_project.1 = bf16[16,64,128]{2,1,0:T(8,128)(2,1)S(1)} custom-call(f32[1]{0:T(128)S(6)} %copy.11.refs_2_.refs_0_, bf16[8,8,640]{2,1,0:T(8,128)(2,1)S(1)} %all_to_all.16.refs_1_, bf16[64,256]{1,0:T(8,128)(2,1)S(1)} %bitcast.10, bf16[64,256]{1,0:T(8,128)(2,1)S(1)} %bitcast.11, bf16[64,512]{1,0:T(8,128)(2,1)S(1)} %bitcast.7, ...), custom_call_target="tpu_custom_call" | custom-call | tf_op jit(solution)/shard_map/combine_project/pallas_call | solution.py:182
  30.1 22.0 %all_to_all.17.shares_ref = bf16[16,64,128]{2,1,0:T(8,128)(2,1)S(1)} all-to-all(bf16[16,64,128]{2,1,0:T(8,128)(2,1)S(1)} %combine_project.1), channel_id=1, replica_groups={{15,13,14,10,12,8,11,6,9,4,7,2,5,1,3,0},{31,29,30,26,28,24,27,22,25,20,..., dimensions={0} | all-to-all | bytes 524288 | tf_op jit(solution)/shard_map/all_to_all | solution.py:192
  52.1 0.6 %sum_heads.1 = bf16[64,128]{1,0:T(8,128)(2,1)} custom-call(bf16[16,64,128]{2,1,0:T(8,128)(2,1)S(1)} %all_to_all.17.shares_ref), custom_call_target="tpu_custom_call" | custom-call | tf_op jit(solution)/shard_map/sum_heads/pallas_call | solution.py:193
Async XLA Ops:
  0.7 17.1 %copy-start.6 = (bf16[8,1,256,512]{3,2,1,0:T(8,128)(2,1)S(1)}, bf16[8,1,256,512]{3,2,1,0:T(8,128)(2,1)}, u32[]{:S(2)}) copy-start(bf16[8,1,256,512]{3,2,1,0:T(8,128)(2,1)} %param.14) | copy-start | bytes 6291460
  17.7 11.5 %copy-start = (bf16[512,2048]{1,0:T(8,128)(2,1)S(1)}, bf16[512,2048]{1,0:T(8,128)(2,1)}, u32[]{:S(2)}) copy-start(bf16[512,2048]{1,0:T(8,128)(2,1)} %refs_7_.1) | copy-start | bytes 6291460
  17.7 11.5 %copy-start.1 = (bf16[8,8,512]{2,1,0:T(8,128)(2,1)S(1)}, bf16[8,8,512]{2,1,0:T(8,128)(2,1)}, u32[]{:S(2)}) copy-start(bf16[8,8,512]{2,1,0:T(8,128)(2,1)} %param.12) | copy-start | bytes 196612
  17.7 11.5 %copy-start.2 = (bf16[8,8,512]{2,1,0:T(8,128)(2,1)S(1)}, bf16[8,8,512]{2,1,0:T(8,128)(2,1)}, u32[]{:S(2)}) copy-start(bf16[8,8,512]{2,1,0:T(8,128)(2,1)} %param.13) | copy-start | bytes 196612
  17.7 11.5 %copy-start.3 = (bf16[8,8,256]{2,1,0:T(8,128)(2,1)S(1)}, bf16[8,8,256]{2,1,0:T(8,128)(2,1)}, u32[]{:S(2)}) copy-start(bf16[8,8,256]{2,1,0:T(8,128)(2,1)} %param.10) | copy-start | bytes 98308
  17.7 11.5 %copy-start.4 = (bf16[8,8,256]{2,1,0:T(8,128)(2,1)S(1)}, bf16[8,8,256]{2,1,0:T(8,128)(2,1)}, u32[]{:S(2)}) copy-start(bf16[8,8,256]{2,1,0:T(8,128)(2,1)} %param.11) | copy-start | bytes 98308
  17.7 11.5 %copy-start.5 = (f32[512]{0:T(512)S(1)}, f32[512]{0:T(512)}, u32[]{:S(2)}) copy-start(f32[512]{0:T(512)} %param.18) | copy-start | bytes 6148

commit v6 on v5

--- a/solution.py
+++ b/solution.py
@@ -102,16 +102,18 @@
     fine = (weights - coarse.astype(F32)).astype(BF16)
     v = v_ref[...]
     carried = back[:, :width].astype(BF16)
-    readout = jnp.dot(jnp.where(one, 1.0, 0.0).astype(BF16), carried, preferred_element_type=F32)
-    readout += jnp.dot(coarse, v, preferred_element_type=F32)
-    readout += jnp.dot(fine, v, preferred_element_type=F32)
+    left = jnp.concatenate([jnp.where(one, 1.0, 0.0).astype(BF16), coarse, fine], axis=1)
+    right = jnp.concatenate([carried, v, v], axis=0)
+    readout = jnp.dot(left, right, preferred_element_type=F32)
     mean = jnp.sum(readout * readout, axis=1, keepdims=True) * (1.0 / width)
     normed = readout * lax.rsqrt(mean + 1e-06) * gain_ref[...] * g_ref[...].astype(F32)
     normed = normed.astype(BF16)
     shares, _, columns = out_ref.shape
-    for share in range(shares):
-        part = jnp.dot(normed, w_ref[:, share * columns : (share + 1) * columns], preferred_element_type=F32)
-        out_ref[HEAD_ORDER.index(share)] = part.astype(out_ref.dtype)
+    for share in range(0, shares, 2):
+        part = jnp.dot(normed, w_ref[:, share * columns : (share + 2) * columns], preferred_element_type=F32)
+        part = part.astype(out_ref.dtype)
+        out_ref[HEAD_ORDER.index(share)] = part[:, 0:columns]
+        out_ref[HEAD_ORDER.index(share + 1)] = part[:, columns:]
 
 
 def total_kernel(shares_ref, out_ref):

time: 53 us -> 53 us (level)
  no operation moved by 1% of the time
where the time goes in v6:
time: 53 us; the launch traced here: 52.7 us
  blocking collectives  48.8 us (92%)
  Pallas kernels  3.12 us (6%)
  between operations  0.74 us (1%)
    all_to_all x1, blocking collectives, shards(): lax.all_to_all(partial, 'heads', 0, 0, axis_index_groups=[list(HEAD_ORDER...  22 us
    all_to_all x1, blocking collectives, shards(): lax.all_to_all(spread, 'rows', 0, 0, axis_index_groups=sources, tiled=True)  16 us
    all_to_all x1, blocking collectives, shards(): lax.all_to_all(readouts, 'rows', 0, 0, axis_index_groups=returns, tiled=T...  10.9 us

profile of v6, /device:TPU:49, one launch (start us, length us, event | category | flops | bytes accessed | tf_op | source)
XLA Modules:
  0.0 52.7 jit_solution(9435957554924869536)
XLA Ops:
  0.7 0.0 copy-start.6
  0.7 1.0 %spread_queries.1 = (bf16[8,64,256]{2,1,0:T(8,128)(2,1)S(1)}, f32[8,8,128]{2,1,0:T(8,128)S(1)}, f32[8,8,128]{2,1,0:T(8,128)S(1)}, f32[8,8,128]{2,1,0:T(8,128)S(1)}) custom-call(s32[8]{0:T(128)} %refs_0_.2, s32[8]{0:T(128)} %refs_1_.1, f32[1]{0:T(128)S(6)} %copy.11.refs_2_.refs_0_, bf16[64,256]{1,0:T(8,128)(2,1)} %bitcast.9), custom_call_target="tpu_custom_call" | custom-call | flops 20000000000 | bytes 262144 | tf_op jit(solution)/shard_map/spread_queries/pallas_call | solution.py:153
  1.7 16.0 %all_to_all.15.refs_0_ = bf16[8,64,256]{2,1,0:T(8,128)(2,1)S(1)} all-to-all(bf16[8,64,256]{2,1,0:T(8,128)(2,1)S(1)} %get-tuple-element.9), channel_id=1, replica_groups={{320,448,64,192,256,384,0,128},{336,464,80,208,272,400,16,144},{352,480..., dimensions={0} | all-to-all | bytes 524288 | tf_op jit(solution)/shard_map/all_to_all | solution.py:172
  17.7 0.0 copy-done.6
  17.7 0.0 copy-start
  17.7 0.0 copy-start.1
  17.7 0.0 copy-start.2
  17.7 0.0 copy-start.3
  17.7 0.0 copy-start.4
  17.7 0.0 copy-start.5
  17.8 0.5 %source_readout.1 = bf16[8,8,640]{2,1,0:T(8,128)(2,1)S(1)} custom-call(bf16[8,64,256]{2,1,0:T(8,128)(2,1)S(1)} %all_to_all.15.refs_0_, bf16[8,256,512]{2,1,0:T(8,128)(2,1)S(1)} %bitcast.13, f32[8,8,128]{2,1,0:T(8,128)S(1)} %get-tuple-element.10.refs_2_, f32[8,8,128]{2,1,0:T(8,128)S(1)} %get-tuple-element.11.refs_3_, f32[8,8,128]{2,1,0:T(8,128)S(1)} %get-tuple-element.12.refs_4_), custom_call_target="tpu_custom_call" | custom-call | flops 20000000000 | bytes 2097152 | tf_op jit(solution)/shard_map/source_readout/pallas_call | solution.py:173
  18.3 10.9 %all_to_all.16.refs_1_ = bf16[8,8,640]{2,1,0:T(8,128)(2,1)S(1)} all-to-all(bf16[8,8,640]{2,1,0:T(8,128)(2,1)S(1)} %source_readout.1), channel_id=1, replica_groups={{320,384,448,0,64,128,192,256},{336,400,464,16,80,144,208,272},{352,416..., dimensions={0} | all-to-all | bytes 163840 | tf_op jit(solution)/shard_map/all_to_all | solution.py:181
  29.2 0.0 copy-done
  29.2 0.0 copy-done.1
  29.2 0.0 copy-done.2
  29.2 0.0 copy-done.3
  29.2 0.0 copy-done.4
  29.2 0.0 copy-done.5
  29.2 0.9 %combine_project.1 = bf16[16,64,128]{2,1,0:T(8,128)(2,1)S(1)} custom-call(f32[1]{0:T(128)S(6)} %copy.11.refs_2_.refs_0_, bf16[8,8,640]{2,1,0:T(8,128)(2,1)S(1)} %all_to_all.16.refs_1_, bf16[64,256]{1,0:T(8,128)(2,1)S(1)} %bitcast.10, bf16[64,256]{1,0:T(8,128)(2,1)S(1)} %bitcast.11, bf16[64,512]{1,0:T(8,128)(2,1)S(1)} %bitcast.7, ...), custom_call_target="tpu_custom_call" | custom-call | tf_op jit(solution)/shard_map/combine_project/pallas_call | solution.py:184
  30.1 22.0 %all_to_all.17.shares_ref = bf16[16,64,128]{2,1,0:T(8,128)(2,1)S(1)} all-to-all(bf16[16,64,128]{2,1,0:T(8,128)(2,1)S(1)} %combine_project.1), channel_id=1, replica_groups={{15,13,14,10,12,8,11,6,9,4,7,2,5,1,3,0},{31,29,30,26,28,24,27,22,25,20,..., dimensions={0} | all-to-all | bytes 524288 | tf_op jit(solution)/shard_map/all_to_all | solution.py:194
  52.1 0.6 %sum_heads.1 = bf16[64,128]{1,0:T(8,128)(2,1)} custom-call(bf16[16,64,128]{2,1,0:T(8,128)(2,1)S(1)} %all_to_all.17.shares_ref), custom_call_target="tpu_custom_call" | custom-call | tf_op jit(solution)/shard_map/sum_heads/pallas_call | solution.py:195
Async XLA Ops:
  0.7 17.1 %copy-start.6 = (bf16[8,1,256,512]{3,2,1,0:T(8,128)(2,1)S(1)}, bf16[8,1,256,512]{3,2,1,0:T(8,128)(2,1)}, u32[]{:S(2)}) copy-start(bf16[8,1,256,512]{3,2,1,0:T(8,128)(2,1)} %param.14) | copy-start | bytes 6291460
  17.7 11.5 %copy-start = (bf16[512,2048]{1,0:T(8,128)(2,1)S(1)}, bf16[512,2048]{1,0:T(8,128)(2,1)}, u32[]{:S(2)}) copy-start(bf16[512,2048]{1,0:T(8,128)(2,1)} %refs_7_.1) | copy-start | bytes 6291460
  17.7 11.5 %copy-start.1 = (bf16[8,8,512]{2,1,0:T(8,128)(2,1)S(1)}, bf16[8,8,512]{2,1,0:T(8,128)(2,1)}, u32[]{:S(2)}) copy-start(bf16[8,8,512]{2,1,0:T(8,128)(2,1)} %param.12) | copy-start | bytes 196612
  17.7 11.5 %copy-start.2 = (bf16[8,8,512]{2,1,0:T(8,128)(2,1)S(1)}, bf16[8,8,512]{2,1,0:T(8,128)(2,1)}, u32[]{:S(2)}) copy-start(bf16[8,8,512]{2,1,0:T(8,128)(2,1)} %param.13) | copy-start | bytes 196612
  17.7 11.5 %copy-start.3 = (bf16[8,8,256]{2,1,0:T(8,128)(2,1)S(1)}, bf16[8,8,256]{2,1,0:T(8,128)(2,1)}, u32[]{:S(2)}) copy-start(bf16[8,8,256]{2,1,0:T(8,128)(2,1)} %param.10) | copy-start | bytes 98308
  17.7 11.5 %copy-start.4 = (bf16[8,8,256]{2,1,0:T(8,128)(2,1)S(1)}, bf16[8,8,256]{2,1,0:T(8,128)(2,1)}, u32[]{:S(2)}) copy-start(bf16[8,8,256]{2,1,0:T(8,128)(2,1)} %param.11) | copy-start | bytes 98308
  17.7 11.5 %copy-start.5 = (f32[512]{0:T(512)S(1)}, f32[512]{0:T(512)}, u32[]{:S(2)}) copy-start(f32[512]{0:T(512)} %param.18) | copy-start | bytes 6148

commit v7 on v6

--- a/solution.py
+++ b/solution.py
@@ -29,10 +29,10 @@
 
 def prepare_kernel(
     spacing, steps, slots, dest_in, step_in, decay_ref, q_in,
-    spread_ref, scale_ref, pick_ref, tail_ref, q_ref, dest_ref, step_ref, sems,
+    spread_ref, scale_ref, pick_ref, tail_ref, dest_ref, step_ref, sems,
 ):
     peers = scale_ref.shape[0]
-    first = pltpu.make_async_copy(q_in, q_ref, sems.at[0])
+    first = pltpu.make_async_copy(q_in, spread_ref.at[0], sems.at[0])
     ints = [
         pltpu.make_async_copy(dest_in, dest_ref, sems.at[1]),
         pltpu.make_async_copy(step_in, step_ref, sems.at[2]),
@@ -40,8 +40,9 @@
     for copy in [first] + ints:
         copy.start()
     first.wait()
-    for peer in range(peers):
-        spread_ref[peer] = q_ref[...]
+    own = spread_ref[0]
+    for peer in range(1, peers):
+        spread_ref[peer] = own
     for copy in ints:
         copy.wait()
     member = lax.div(lax.axis_index("rows"), spacing)
@@ -162,7 +163,6 @@
         [ANY, ANY, SMEM, ANY],
         (VMEM,) * 4,
         [
-            pltpu.VMEM(q.shape, BF16),
             pltpu.SMEM(dest_slot.shape, jnp.int32),
             pltpu.SMEM(arrive_step.shape, jnp.int32),
             pltpu.SemaphoreType.DMA((3,)),

time: 53 us -> 53 us (level)
  no operation moved by 1% of the time
where the time goes in v7:
time: 53 us; the launch traced here: 52.7 us
  blocking collectives  48.8 us (92%)
  Pallas kernels  3.12 us (6%)
  between operations  0.74 us (1%)
    all_to_all x1, blocking collectives, shards(): lax.all_to_all(partial, 'heads', 0, 0, axis_index_groups=[list(HEAD_ORDER...  22 us
    all_to_all x1, blocking collectives, shards(): lax.all_to_all(spread, 'rows', 0, 0, axis_index_groups=sources, tiled=True)  16 us
    all_to_all x1, blocking collectives, shards(): lax.all_to_all(readouts, 'rows', 0, 0, axis_index_groups=returns, tiled=T...  10.9 us

profile of v7, /device:TPU:49, one launch (start us, length us, event | category | flops | bytes accessed | tf_op | source)
XLA Modules:
  0.0 52.7 jit_solution(17972074353994733042)
XLA Ops:
  0.7 0.0 copy-start.6
  0.7 1.0 %spread_queries.1 = (bf16[8,64,256]{2,1,0:T(8,128)(2,1)S(1)}, f32[8,8,128]{2,1,0:T(8,128)S(1)}, f32[8,8,128]{2,1,0:T(8,128)S(1)}, f32[8,8,128]{2,1,0:T(8,128)S(1)}) custom-call(s32[8]{0:T(128)} %refs_0_.2, s32[8]{0:T(128)} %refs_1_.1, f32[1]{0:T(128)S(6)} %copy.11.refs_2_.refs_0_, bf16[64,256]{1,0:T(8,128)(2,1)} %bitcast.9), custom_call_target="tpu_custom_call" | custom-call | flops 20000000000 | bytes 262144 | tf_op jit(solution)/shard_map/spread_queries/pallas_call | solution.py:154
  1.7 16.0 %all_to_all.15.refs_0_ = bf16[8,64,256]{2,1,0:T(8,128)(2,1)S(1)} all-to-all(bf16[8,64,256]{2,1,0:T(8,128)(2,1)S(1)} %get-tuple-element.9), channel_id=1, replica_groups={{320,448,64,192,256,384,0,128},{336,464,80,208,272,400,16,144},{352,480..., dimensions={0} | all-to-all | bytes 524288 | tf_op jit(solution)/shard_map/all_to_all | solution.py:172
  17.7 0.0 copy-done.6
  17.7 0.0 copy-start
  17.7 0.0 copy-start.1
  17.7 0.0 copy-start.2
  17.7 0.0 copy-start.3
  17.7 0.0 copy-start.4
  17.7 0.0 copy-start.5
  17.8 0.5 %source_readout.1 = bf16[8,8,640]{2,1,0:T(8,128)(2,1)S(1)} custom-call(bf16[8,64,256]{2,1,0:T(8,128)(2,1)S(1)} %all_to_all.15.refs_0_, bf16[8,256,512]{2,1,0:T(8,128)(2,1)S(1)} %bitcast.13, f32[8,8,128]{2,1,0:T(8,128)S(1)} %get-tuple-element.10.refs_2_, f32[8,8,128]{2,1,0:T(8,128)S(1)} %get-tuple-element.11.refs_3_, f32[8,8,128]{2,1,0:T(8,128)S(1)} %get-tuple-element.12.refs_4_), custom_call_target="tpu_custom_call" | custom-call | flops 20000000000 | bytes 2097152 | tf_op jit(solution)/shard_map/source_readout/pallas_call | solution.py:173
  18.3 10.9 %all_to_all.16.refs_1_ = bf16[8,8,640]{2,1,0:T(8,128)(2,1)S(1)} all-to-all(bf16[8,8,640]{2,1,0:T(8,128)(2,1)S(1)} %source_readout.1), channel_id=1, replica_groups={{320,384,448,0,64,128,192,256},{336,400,464,16,80,144,208,272},{352,416..., dimensions={0} | all-to-all | bytes 163840 | tf_op jit(solution)/shard_map/all_to_all | solution.py:181
  29.2 0.0 copy-done
  29.2 0.0 copy-done.1
  29.2 0.0 copy-done.2
  29.2 0.0 copy-done.3
  29.2 0.0 copy-done.4
  29.2 0.0 copy-done.5
  29.2 0.9 %combine_project.1 = bf16[16,64,128]{2,1,0:T(8,128)(2,1)S(1)} custom-call(f32[1]{0:T(128)S(6)} %copy.11.refs_2_.refs_0_, bf16[8,8,640]{2,1,0:T(8,128)(2,1)S(1)} %all_to_all.16.refs_1_, bf16[64,256]{1,0:T(8,128)(2,1)S(1)} %bitcast.10, bf16[64,256]{1,0:T(8,128)(2,1)S(1)} %bitcast.11, bf16[64,512]{1,0:T(8,128)(2,1)S(1)} %bitcast.7, ...), custom_call_target="tpu_custom_call" | custom-call | tf_op jit(solution)/shard_map/combine_project/pallas_call | solution.py:184
  30.1 22.0 %all_to_all.17.shares_ref = bf16[16,64,128]{2,1,0:T(8,128)(2,1)S(1)} all-to-all(bf16[16,64,128]{2,1,0:T(8,128)(2,1)S(1)} %combine_project.1), channel_id=1, replica_groups={{15,13,14,10,12,8,11,6,9,4,7,2,5,1,3,0},{31,29,30,26,28,24,27,22,25,20,..., dimensions={0} | all-to-all | bytes 524288 | tf_op jit(solution)/shard_map/all_to_all | solution.py:194
  52.1 0.6 %sum_heads.1 = bf16[64,128]{1,0:T(8,128)(2,1)} custom-call(bf16[16,64,128]{2,1,0:T(8,128)(2,1)S(1)} %all_to_all.17.shares_ref), custom_call_target="tpu_custom_call" | custom-call | tf_op jit(solution)/shard_map/sum_heads/pallas_call | solution.py:195
Async XLA Ops:
  0.7 17.1 %copy-start.6 = (bf16[8,1,256,512]{3,2,1,0:T(8,128)(2,1)S(1)}, bf16[8,1,256,512]{3,2,1,0:T(8,128)(2,1)}, u32[]{:S(2)}) copy-start(bf16[8,1,256,512]{3,2,1,0:T(8,128)(2,1)} %param.14) | copy-start | bytes 6291460
  17.7 11.5 %copy-start = (bf16[512,2048]{1,0:T(8,128)(2,1)S(1)}, bf16[512,2048]{1,0:T(8,128)(2,1)}, u32[]{:S(2)}) copy-start(bf16[512,2048]{1,0:T(8,128)(2,1)} %refs_7_.1) | copy-start | bytes 6291460
  17.7 11.5 %copy-start.1 = (bf16[8,8,512]{2,1,0:T(8,128)(2,1)S(1)}, bf16[8,8,512]{2,1,0:T(8,128)(2,1)}, u32[]{:S(2)}) copy-start(bf16[8,8,512]{2,1,0:T(8,128)(2,1)} %param.12) | copy-start | bytes 196612
  17.7 11.5 %copy-start.2 = (bf16[8,8,512]{2,1,0:T(8,128)(2,1)S(1)}, bf16[8,8,512]{2,1,0:T(8,128)(2,1)}, u32[]{:S(2)}) copy-start(bf16[8,8,512]{2,1,0:T(8,128)(2,1)} %param.13) | copy-start | bytes 196612
  17.7 11.5 %copy-start.3 = (bf16[8,8,256]{2,1,0:T(8,128)(2,1)S(1)}, bf16[8,8,256]{2,1,0:T(8,128)(2,1)}, u32[]{:S(2)}) copy-start(bf16[8,8,256]{2,1,0:T(8,128)(2,1)} %param.10) | copy-start | bytes 98308
  17.7 11.5 %copy-start.4 = (bf16[8,8,256]{2,1,0:T(8,128)(2,1)S(1)}, bf16[8,8,256]{2,1,0:T(8,128)(2,1)}, u32[]{:S(2)}) copy-start(bf16[8,8,256]{2,1,0:T(8,128)(2,1)} %param.11) | copy-start | bytes 98308
  17.7 11.5 %copy-start.5 = (f32[512]{0:T(512)S(1)}, f32[512]{0:T(512)}, u32[]{:S(2)}) copy-start(f32[512]{0:T(512)} %param.18) | copy-start | bytes 6148

commit v8 on v7

--- a/solution.py
+++ b/solution.py
@@ -13,7 +13,7 @@
 TAIL = 128
 SOURCE_ORDER = (5, 7, 1, 3, 4, 6, 0, 2)
 RETURN_ORDER = (5, 6, 7, 0, 1, 2, 3, 4)
-HEAD_ORDER = (15, 13, 14, 10, 12, 8, 11, 6, 9, 4, 7, 2, 5, 1, 3, 0)
+HEAD_ORDER = (15, 12, 14, 10, 13, 8, 11, 6, 9, 4, 7, 2, 5, 0, 3, 1)
 
 
 def in_hbm(value):

time: 53 us -> 52.9 us (level)
  the two profiles are of different devices: /device:TPU:49 before, /device:TPU:113 now
where the time goes in v8:
time: 52.9 us; the launch traced here: 52.6 us
  blocking collectives  48.8 us (92%)
  Pallas kernels  3.11 us (6%)
  between operations  0.74 us (1%)
    all_to_all x1, blocking collectives, shards(): lax.all_to_all(partial, 'heads', 0, 0, axis_index_groups=[list(HEAD_ORDER...  19.7 us
    all_to_all x1, blocking collectives, shards(): lax.all_to_all(spread, 'rows', 0, 0, axis_index_groups=sources, tiled=True)  17.4 us
    all_to_all x1, blocking collectives, shards(): lax.all_to_all(readouts, 'rows', 0, 0, axis_index_groups=returns, tiled=T...  11.6 us

profile of v8, /device:TPU:113, one launch (start us, length us, event | category | flops | bytes accessed | tf_op | source)
XLA Modules:
  0.0 52.6 jit_solution(12448262529976582178)
XLA Ops:
  0.7 0.0 copy-start.6
  0.7 1.0 %spread_queries.1 = (bf16[8,64,256]{2,1,0:T(8,128)(2,1)S(1)}, f32[8,8,128]{2,1,0:T(8,128)S(1)}, f32[8,8,128]{2,1,0:T(8,128)S(1)}, f32[8,8,128]{2,1,0:T(8,128)S(1)}) custom-call(s32[8]{0:T(128)} %refs_0_.2, s32[8]{0:T(128)} %refs_1_.1, f32[1]{0:T(128)S(6)} %copy.11.refs_2_.refs_0_, bf16[64,256]{1,0:T(8,128)(2,1)} %bitcast.9), custom_call_target="tpu_custom_call" | custom-call | flops 20000000000 | bytes 262144 | tf_op jit(solution)/shard_map/spread_queries/pallas_call | solution.py:154
  1.7 17.4 %all_to_all.15.refs_0_ = bf16[8,64,256]{2,1,0:T(8,128)(2,1)S(1)} all-to-all(bf16[8,64,256]{2,1,0:T(8,128)(2,1)S(1)} %get-tuple-element.9), channel_id=1, replica_groups={{320,448,64,192,256,384,0,128},{336,464,80,208,272,400,16,144},{352,480..., dimensions={0} | all-to-all | bytes 524288 | tf_op jit(solution)/shard_map/all_to_all | solution.py:172
  19.1 0.0 copy-done.6
  19.1 0.0 copy-start
  19.1 0.0 copy-start.1
  19.1 0.0 copy-start.2
  19.1 0.0 copy-start.3
  19.1 0.0 copy-start.4
  19.1 0.0 copy-start.5
  19.2 0.5 %source_readout.1 = bf16[8,8,640]{2,1,0:T(8,128)(2,1)S(1)} custom-call(bf16[8,64,256]{2,1,0:T(8,128)(2,1)S(1)} %all_to_all.15.refs_0_, bf16[8,256,512]{2,1,0:T(8,128)(2,1)S(1)} %bitcast.13, f32[8,8,128]{2,1,0:T(8,128)S(1)} %get-tuple-element.10.refs_2_, f32[8,8,128]{2,1,0:T(8,128)S(1)} %get-tuple-element.11.refs_3_, f32[8,8,128]{2,1,0:T(8,128)S(1)} %get-tuple-element.12.refs_4_), custom_call_target="tpu_custom_call" | custom-call | flops 20000000000 | bytes 2097152 | tf_op jit(solution)/shard_map/source_readout/pallas_call | solution.py:173
  19.7 11.6 %all_to_all.16.refs_1_ = bf16[8,8,640]{2,1,0:T(8,128)(2,1)S(1)} all-to-all(bf16[8,8,640]{2,1,0:T(8,128)(2,1)S(1)} %source_readout.1), channel_id=1, replica_groups={{320,384,448,0,64,128,192,256},{336,400,464,16,80,144,208,272},{352,416..., dimensions={0} | all-to-all | bytes 163840 | tf_op jit(solution)/shard_map/all_to_all | solution.py:181
  31.3 0.0 copy-done
  31.3 0.0 copy-done.1
  31.3 0.0 copy-done.2
  31.3 0.0 copy-done.3
  31.3 0.0 copy-done.4
  31.3 0.0 copy-done.5
  31.4 0.9 %combine_project.1 = bf16[16,64,128]{2,1,0:T(8,128)(2,1)S(1)} custom-call(f32[1]{0:T(128)S(6)} %copy.11.refs_2_.refs_0_, bf16[8,8,640]{2,1,0:T(8,128)(2,1)S(1)} %all_to_all.16.refs_1_, bf16[64,256]{1,0:T(8,128)(2,1)S(1)} %bitcast.10, bf16[64,256]{1,0:T(8,128)(2,1)S(1)} %bitcast.11, bf16[64,512]{1,0:T(8,128)(2,1)S(1)} %bitcast.7, ...), custom_call_target="tpu_custom_call" | custom-call | tf_op jit(solution)/shard_map/combine_project/pallas_call | solution.py:184
  32.3 19.7 %all_to_all.17.shares_ref = bf16[16,64,128]{2,1,0:T(8,128)(2,1)S(1)} all-to-all(bf16[16,64,128]{2,1,0:T(8,128)(2,1)S(1)} %combine_project.1), channel_id=1, replica_groups={{15,12,14,10,13,8,11,6,9,4,7,2,5,0,3,1},{31,28,30,26,29,24,27,22,25,20,..., dimensions={0} | all-to-all | bytes 524288 | tf_op jit(solution)/shard_map/all_to_all | solution.py:194
  52.0 0.6 %sum_heads.1 = bf16[64,128]{1,0:T(8,128)(2,1)} custom-call(bf16[16,64,128]{2,1,0:T(8,128)(2,1)S(1)} %all_to_all.17.shares_ref), custom_call_target="tpu_custom_call" | custom-call | tf_op jit(solution)/shard_map/sum_heads/pallas_call | solution.py:195
Async XLA Ops:
  0.7 18.5 %copy-start.6 = (bf16[8,1,256,512]{3,2,1,0:T(8,128)(2,1)S(1)}, bf16[8,1,256,512]{3,2,1,0:T(8,128)(2,1)}, u32[]{:S(2)}) copy-start(bf16[8,1,256,512]{3,2,1,0:T(8,128)(2,1)} %param.14) | copy-start | bytes 6291460
  19.1 12.2 %copy-start = (bf16[512,2048]{1,0:T(8,128)(2,1)S(1)}, bf16[512,2048]{1,0:T(8,128)(2,1)}, u32[]{:S(2)}) copy-start(bf16[512,2048]{1,0:T(8,128)(2,1)} %refs_7_.1) | copy-start | bytes 6291460
  19.1 12.2 %copy-start.1 = (bf16[8,8,512]{2,1,0:T(8,128)(2,1)S(1)}, bf16[8,8,512]{2,1,0:T(8,128)(2,1)}, u32[]{:S(2)}) copy-start(bf16[8,8,512]{2,1,0:T(8,128)(2,1)} %param.12) | copy-start | bytes 196612
  19.1 12.2 %copy-start.2 = (bf16[8,8,512]{2,1,0:T(8,128)(2,1)S(1)}, bf16[8,8,512]{2,1,0:T(8,128)(2,1)}, u32[]{:S(2)}) copy-start(bf16[8,8,512]{2,1,0:T(8,128)(2,1)} %param.13) | copy-start | bytes 196612
  19.1 12.2 %copy-start.3 = (bf16[8,8,256]{2,1,0:T(8,128)(2,1)S(1)}, bf16[8,8,256]{2,1,0:T(8,128)(2,1)}, u32[]{:S(2)}) copy-start(bf16[8,8,256]{2,1,0:T(8,128)(2,1)} %param.10) | copy-start | bytes 98308
  19.1 12.2 %copy-start.4 = (bf16[8,8,256]{2,1,0:T(8,128)(2,1)S(1)}, bf16[8,8,256]{2,1,0:T(8,128)(2,1)}, u32[]{:S(2)}) copy-start(bf16[8,8,256]{2,1,0:T(8,128)(2,1)} %param.11) | copy-start | bytes 98308
  19.1 12.2 %copy-start.5 = (f32[512]{0:T(512)S(1)}, f32[512]{0:T(512)}, u32[]{:S(2)}) copy-start(f32[512]{0:T(512)} %param.18) | copy-start | bytes 6148
